TPU v7x, 32 devices: a whole 2x2x4 slice. The times are simulated.
32 devices in a mesh: dp: 4 (over y, x), expert: 4 (over z), tensor: 2 (over core).
Axes of the slice: x: 2, y: 2, z: 4, core: 2. Of those that a mesh axis runs over, the one named last changes fastest.
Arguments:
- out_grad: bfloat16 [2048, 3584], P(('dp', 'expert'), 'tensor'), may hold values from -6 to 6
- routing: int32 [2048, 8], P(('dp', 'expert')), may hold values from 0 to 15, all different within a row; in each aligned block of 128 rows (0 to 127, 128 to 255, ...) at most 128 rows name the same one
- route_probs: float32 [2048, 8], P(('dp', 'expert')), may hold values from 0.05 to 1
- w_down: bfloat16 [4, 3584, 1024], P('expert', 'dp', 'tensor'), may hold values from -0.1875 to 0.1875
- saved_gate: bfloat16 [8192, 1024], P(('dp', 'expert'), 'tensor'), may hold values from -8 to 8
- saved_up: bfloat16 [8192, 1024], P(('dp', 'expert'), 'tensor'), may hold values from -6 to 6
Outputs:
- weight_grad: bfloat16 [4, 3584, 1024], P('expert', 'dp', 'tensor')
- grad_gate: bfloat16 [8192, 1024], P(('dp', 'expert'), 'tensor')
- grad_up: bfloat16 [8192, 1024], P(('dp', 'expert'), 'tensor')
- grad_amax: float32 [4, 4], P('dp', 'expert')
Inputs may be any that keep to these rules, and one draw needn't show every extreme that they name: `routing`: each row names 8 different experts; in the rows of one device no expert is named more than 128 times.
All inputs are finite; a program needn't handle non-finite values. Where the computation divides by a largest or mean magnitude, that divisor is 1e-20 or more.
Results may differ from a plain program's by a relative error of at most 0.009.
Values may be sent and summed in bfloat16 or wider, within the bound.
No kernel may reach another device: no remote copies, remote signals or barrier semaphores. Data moves between devices by JAX's collectives and lax.ppermute only.
A program may use at most 64 MiB of HBM per device.

v0:
```python
import jax
import jax.numpy as jnp
from jax import lax
from jax.sharding import PartitionSpec as P

epsilon = 1e-06


def slot_tables(routing, route_probs, owners, capacity):
    tok_count = routing.shape[0]
    matches = routing[:, :, None] == jnp.arange(owners, dtype=jnp.int32)[None, None, :]
    is_routed = jnp.any(matches, axis=1).astype(jnp.int32)
    scaling = jnp.sum(jnp.where(matches, route_probs[:, :, None], 0.0), axis=1)
    slot_rank = jnp.cumsum(is_routed, axis=0) - is_routed
    picked = (is_routed[:, :, None] == 1) & (
        slot_rank[:, :, None] == jnp.arange(capacity, dtype=jnp.int32)[None, None, :]
    )
    token_ids = jnp.arange(tok_count, dtype=jnp.int32)[:, None, None]
    slot_token = jnp.sum(jnp.where(picked, token_ids, 0), axis=0)
    slot_scale = jnp.sum(jnp.where(picked, scaling[:, :, None], 0.0), axis=0)
    return (slot_token, slot_scale)


def body(out_grad, routing, route_probs, w_down, saved_gate, saved_up):
    owners = lax.axis_size("expert")
    slot_count = saved_gate.shape[0]
    capacity = slot_count // owners
    slot_token, slot_scale = slot_tables(routing, route_probs, owners, capacity)
    features = lax.all_gather(out_grad, "tensor", axis=1, tiled=True)
    picked_rows = jnp.take(features, slot_token, axis=0)
    arrived = lax.all_to_all(
        (picked_rows.astype(jnp.float32) * slot_scale[:, :, None]).astype(jnp.bfloat16),
        "expert",
        split_axis=0,
        concat_axis=0,
        tiled=True,
    )
    slot_rows = arrived.reshape(slot_count, features.shape[1])
    columns = slot_rows
    grad_hidden = jnp.dot(
        columns,
        lax.all_gather(w_down, "dp", axis=1, tiled=True)[0],
        preferred_element_type=jnp.float32,
    )
    gate_pre = saved_gate.astype(jnp.float32)
    up_pre = saved_up.astype(jnp.float32)
    sigmoid_gate = jax.nn.sigmoid(gate_pre)
    silu_gate = gate_pre * sigmoid_gate
    activation = (silu_gate * up_pre).astype(jnp.bfloat16)
    grad_amax = lax.pmax(jnp.max(jnp.abs(grad_hidden)), "tensor")
    columns = slot_rows
    weight_sum = lax.psum_scatter(
        lax.dot_general(
            columns, activation, (((0,), (0,)), ((), ())), preferred_element_type=jnp.float32
        ).astype(jnp.bfloat16),
        "dp",
        scatter_dimension=0,
        tiled=True,
    )
    quantized = lax.optimization_barrier(
        (grad_hidden / (grad_amax + epsilon)).astype(jnp.bfloat16)
    ).astype(jnp.float32)
    grad_gate = (
        quantized * up_pre * sigmoid_gate * (1.0 + gate_pre * (1.0 - sigmoid_gate))
    ).astype(jnp.bfloat16)
    grad_up = (quantized * silu_gate).astype(jnp.bfloat16)
    weight_grad = weight_sum.reshape(w_down.shape)
    return (weight_grad, grad_gate, grad_up, grad_amax.reshape(1, 1))


def solution(mesh):
    placed = (
        P(("dp", "expert"), "tensor"),
        P(("dp", "expert"), None),
        P(("dp", "expert"), None),
        P("expert", "dp", "tensor"),
        P(("dp", "expert"), "tensor"),
        P(("dp", "expert"), "tensor"),
    )
    return jax.shard_map(
        body,
        mesh=mesh,
        in_specs=placed,
        out_specs=(
            P("expert", "dp", "tensor"),
            P(("dp", "expert"), "tensor"),
            P(("dp", "expert"), "tensor"),
            P("dp", "expert"),
        ),
        check_vma=False,
    )
```

profile of v0, /device:TPU:0, one launch (start us, length us, event | category | flops | bytes accessed | tf_op | source)
XLA Modules:
  0.0 171.9 jit_solution(10410794477552787552)
XLA Ops:
  7.2 0.7 fusion.13
  7.9 0.1 copy.16
  8.0 0.2 reduce_window_sum.11
  8.2 0.1 copy.17
  8.2 0.2 select_reduce_fusion.1
  8.5 2.8 %all_gather.6 = bf16[128,3584]{1,0:T(8,128)(2,1)S(1)} all-gather(bf16[128,1792]{1,0:T(8,128)(2,1)} %param.6), channel_id=1, replica_groups=mesh['dp'=4,'expert'=4,'tensor'=2] {'tensor'}, dimensions={1}, use_global_device_ids=true | all-gather | bytes 1376256 | tf_op jit(solution)/shard_map/all_gather | solution.py:29
  11.3 0.7 select_reduce_fusion.2
  12.0 0.3 select_reduce_fusion
  12.3 4.2 %gather_fusion = bf16[512,3584]{1,0:T(8,128)(2,1)} fusion(bf16[128,3584]{1,0:T(8,128)(2,1)S(1)} %all_gather.6, s32[1024]{0:T(1024)S(1)} %pad_clamp_fusion), kind=kCustom, calls=%fused_computation | custom fusion | bytes 7342080 | tf_op jit(solution)/shard_map/jit(_take)/gather | solution.py:30
  16.4 6.0 %multiply_convert_fusion = bf16[4,128,3584]{2,1,0:T(8,128)(2,1)} fusion(f32[4,128]{1,0:T(4,128)S(1)} %select_reduce_fusion, bf16[4,128,3584]{2,1,0:T(8,128)(2,1)} %bitcast.15, pred[4,128]{1,0:T(4,128)(4,1)S(1)} %compare_and_fusion), kind=kLoop, calls=%fused_computation.1 | loop fusion | flops 7340032 | bytes 7342592 | tf_op jit(solution)/shard_map/convert_element_type | solution.py:32
  22.4 0.0 copy-start
  22.4 0.0 copy-start.1
  22.4 6.4 %all-to-all-start = ((bf16[4,128,3584]{2,1,0:T(8,128)(2,1)}), bf16[4,128,3584]{2,1,0:T(8,128)(2,1)}, u32[]{:S(2)}, u32[]{:S(2)}) async-start(bf16[4,128,3584]{2,1,0:T(8,128)(2,1)} %multiply_convert_fusion), calls=%async_computation | async-start | bytes 7340032 | tf_op jit(solution)/shard_map/all_to_all | solution.py:31
  28.8 0.0 all-gather.2.cloned.1.call-start
  28.8 0.7 all-gather.2.cloned.1.call-update
  29.5 0.0 reduce-scatter.2.cloned.1.call-start
  29.6 81.6 %all-to-all-done = bf16[4,128,3584]{2,1,0:T(8,128)(2,1)} async-done(((bf16[4,128,3584]{2,1,0:T(8,128)(2,1)}), bf16[4,128,3584]{2,1,0:T(8,128)(2,1)}, u32[]{:S(2)}, u32[]{:S(2)}) %all-to-all-start) | async-done | bytes 3670048 | tf_op jit(solution)/shard_map/all_to_all | solution.py:31
  111.2 0.0 copy-done
  111.2 0.0 copy-done.1
  111.2 6.2 %convolution_convert_fusion = bf16[3584,512]{1,0:T(8,128)(2,1)} fusion(bf16[512,3584]{1,0:T(8,128)(2,1)} %bitcast.3, bf16[512,512]{1,0:T(8,128)(2,1)S(1)} %copy-done, bf16[512,512]{1,0:T(8,128)(2,1)S(1)} %copy-done.1), kind=kOutput, calls=%fused_computation.2 | convolution fusion | flops 1882980352 | bytes 8388608 | tf_op jit(solution)/shard_map/dot_general | solution.py:53
  117.4 0.0 reduce-scatter.2.cloned.1.call-update
  117.4 0.0 all-gather.2.cloned.1.call-done
  117.4 5.9 %abs_reduce_fusion = (f32[]{:T(128)}, f32[512,512]{1,0:T(8,128)S(1)}) fusion(bf16[512,3584]{1,0:T(8,128)(2,1)} %bitcast.3, bf16[1,3584,512]{2,1,0:T(8,128)(2,1)} %all-gather.2.cloned.1.call-done), kind=kOutput, calls=%fused_computation.21 | convolution fusion | flops 1879572480 | bytes 8388612 | tf_op jit(solution)/shard_map/dot_general | solution.py:40
  123.3 3.1 %pmax.7 = f32[]{:T(128)} all-reduce(f32[]{:T(128)} %get-tuple-element.8), channel_id=1, replica_groups=mesh['dp'=4,'expert'=4,'tensor'=2] {'tensor'}, use_global_device_ids=true, to_apply=%region_7.8 | all-reduce | flops 1 | bytes 8 | tf_op jit(solution)/shard_map/pmax | solution.py:50
  127.0 0.1 divide_convert_fusion
  127.1 1.5 fusion.6
  128.7 36.4 %reduce-scatter.2.cloned.1.call-done = bf16[896,512]{1,0:T(8,128)(2,1)} async-done(((bf16[3584,512]{1,0:T(8,128)(2,1)}), bf16[896,512]{1,0:T(8,128)(2,1)}) %reduce-scatter.2.cloned.1.call-update) | async-done | bytes 917520 | tf_op jit(solution)/shard_map/reduce_scatter | solution.py:52
  (5 shorter events, 0.0 us)
Async XLA Ops:
  22.4 88.8 %copy-start = (bf16[512,512]{1,0:T(8,128)(2,1)S(1)}, bf16[512,512]{1,0:T(8,128)(2,1)}, u32[]{:S(2)}) copy-start(bf16[512,512]{1,0:T(8,128)(2,1)} %param.11) | copy-start | bytes 1572868
  22.4 88.8 %copy-start.1 = (bf16[512,512]{1,0:T(8,128)(2,1)S(1)}, bf16[512,512]{1,0:T(8,128)(2,1)}, u32[]{:S(2)}) copy-start(bf16[512,512]{1,0:T(8,128)(2,1)} %param.10) | copy-start | bytes 1572868
  22.4 88.8 %all-to-all-start = ((bf16[4,128,3584]{2,1,0:T(8,128)(2,1)}), bf16[4,128,3584]{2,1,0:T(8,128)(2,1)}, u32[]{:S(2)}, u32[]{:S(2)}) async-start(bf16[4,128,3584]{2,1,0:T(8,128)(2,1)} %multiply_convert_fusion), calls=%async_computation | async-start | bytes 7340032 | tf_op jit(solution)/shard_map/all_to_all | solution.py:31
  28.8 88.6 %all-gather.2.cloned.1.call-start = ((), (), s32[]{:S(2)}) async-start(), calls=%async_computation.3 | async-start | bytes 4587520 | tf_op jit(solution)/shard_map/all_gather | solution.py:42
  29.5 135.5 %reduce-scatter.2.cloned.1.call-start = ((), (), s32[]{:S(2)}) async-start(), calls=%async_computation.2 | async-start | bytes 4587520 | tf_op jit(solution)/shard_map/reduce_scatter | solution.py:52
Sparse Core Ops, SparseCore 0:
  31.5 49.8 all-gather.1
  117.5 47.4 reduce-scatter.1
where the time goes:
time: 172 us
  waiting for transfers between devices  119 us (69%)
  between operations  14.7 us (9%)
  matrix products  12 us (7%)
  other arithmetic  9.81 us (6%)
  starting transfers between devices  6.41 us (4%)
  blocking collectives  5.83 us (3%)
  local copies, waits for them, and re-layouts  4.33 us (3%)
    all_to_all x1, waiting for transfers between devices, body(): lax.all_to_all((picked_rows.astype(jnp.float32) * slot_scale[:, :, None])...  81.6 us
    reduce_scatter x1, waiting for transfers between devices, body(): lax.psum_scatter(lax.dot_general(columns, activation, (((0,), (0,)), ((),...  36.4 us
    all_to_all x1, starting transfers between devices, body(): lax.all_to_all((picked_rows.astype(jnp.float32) * slot_scale[:, :, None])...  6.37 us
    dot_general x1, matrix products, body(): lax.dot_general(columns, activation, (((0,), (0,)), ((), ())), preferred_...  6.16 us
    convert_element_type x1, other arithmetic, body(): (picked_rows.astype(jnp.float32) * slot_scale[:, :, None]).astype(jnp.bfl...  6.01 us
    dot_general x1, matrix products, body(): jnp.dot(columns, lax.all_gather(w_down, 'dp', axis=1, tiled=True)[0], pre...  5.85 us
    gather x1, local copies, waits for them, and re-layouts, body(): picked_rows = jnp.take(features, slot_token, axis=0)  4.15 us
  transfers between devices with their start and end apart: 3, of which 2 were waited for; matrix products, arithmetic and copies ran while one was open for 8% of the time, Pallas kernels for 0%

commit v1 on v0

v1 whole, which is shorter than its diff:
```python
import jax
import jax.numpy as jnp
from jax import lax
from jax.sharding import PartitionSpec as P

epsilon = 1e-06


def ranks(flags):
    rows = flags.shape[0]
    at = lax.broadcasted_iota(jnp.int32, (rows, rows), 0)
    before = lax.broadcasted_iota(jnp.int32, (rows, rows), 1) < at
    counts = jnp.dot(
        before.astype(jnp.bfloat16), flags.astype(jnp.bfloat16), preferred_element_type=jnp.float32
    )
    return counts.astype(jnp.int32)


def route(routing, route_probs, owners):
    matches = routing[:, :, None] == jnp.arange(owners, dtype=jnp.int32)[None, None, :]
    is_routed = jnp.any(matches, axis=1)
    scaling = jnp.sum(jnp.where(matches, route_probs[:, :, None], 0.0), axis=1)
    return is_routed, scaling, ranks(is_routed)


def by_slots(out_grad, routing, route_probs, w_down, saved_gate, saved_up):
    owners = lax.axis_size("expert")
    slot_count = saved_gate.shape[0]
    capacity = slot_count // owners
    is_routed, scaling, slot_rank = route(routing, route_probs, owners)
    picked = is_routed[:, :, None] & (
        slot_rank[:, :, None] == jnp.arange(capacity, dtype=jnp.int32)[None, None, :]
    )
    token_ids = jnp.arange(routing.shape[0], dtype=jnp.int32)[:, None, None]
    slot_token = jnp.sum(jnp.where(picked, token_ids, 0), axis=0)
    slot_scale = jnp.sum(jnp.where(picked, scaling[:, :, None], 0.0), axis=0)
    picked_rows = jnp.take(out_grad, slot_token, axis=0)
    arrived = lax.all_to_all(
        (picked_rows.astype(jnp.float32) * slot_scale[:, :, None]).astype(jnp.bfloat16),
        "expert",
        split_axis=0,
        concat_axis=0,
        tiled=True,
    )
    slot_rows = lax.all_gather(
        arrived.reshape(slot_count, out_grad.shape[1]), "tensor", axis=1, tiled=True
    )
    grad_hidden = jnp.dot(
        slot_rows,
        lax.all_gather(w_down, "dp", axis=1, tiled=True)[0],
        preferred_element_type=jnp.float32,
    )
    gate_pre = saved_gate.astype(jnp.float32)
    up_pre = saved_up.astype(jnp.float32)
    sigmoid_gate = jax.nn.sigmoid(gate_pre)
    silu_gate = gate_pre * sigmoid_gate
    activation = (silu_gate * up_pre).astype(jnp.bfloat16)
    grad_amax = lax.pmax(jnp.max(jnp.abs(grad_hidden)), "tensor")
    weight_sum = lax.psum_scatter(
        lax.dot_general(
            slot_rows, activation, (((0,), (0,)), ((), ())), preferred_element_type=jnp.float32
        ).astype(jnp.bfloat16),
        "dp",
        scatter_dimension=0,
        tiled=True,
    )
    quantized = (grad_hidden / (grad_amax + epsilon)).astype(jnp.bfloat16).astype(jnp.float32)
    grad_gate = (
        quantized * up_pre * sigmoid_gate * (1.0 + gate_pre * (1.0 - sigmoid_gate))
    ).astype(jnp.bfloat16)
    grad_up = (quantized * silu_gate).astype(jnp.bfloat16)
    return (weight_sum.reshape(w_down.shape), grad_gate, grad_up, grad_amax.reshape(1, 1))


def by_tokens(out_grad, routing, route_probs, w_down, saved_gate, saved_up):
    n_dp, owners, cores = (lax.axis_size(a) for a in ("dp", "expert", "tensor"))
    p, e, t = (lax.axis_index(a) for a in ("dp", "expert", "tensor"))
    tokens = routing.shape[0]
    depth, hidden = w_down.shape[1:]
    slot_count = saved_gate.shape[0]
    capacity = slot_count // owners
    per_core = n_dp // cores
    weight = w_down[0]

    def turn(k):
        return [(s, (s + k) % owners) for s in range(owners)]

    is_routed, scaling, slot_rank = route(routing, route_probs, owners)
    slot_of = jnp.where(is_routed, e * capacity + slot_rank, -1).astype(jnp.float32)
    tables = jnp.stack([slot_of.T, scaling.T], axis=1)
    got = [
        lax.ppermute(lax.dynamic_index_in_dim(tables, (e + k) % owners, 0, keepdims=False), "expert", turn(k))
        if k
        else lax.dynamic_index_in_dim(tables, e, 0, keepdims=False)
        for k in range(owners)
    ]
    got = jnp.stack(got, axis=1)

    chunks = CHUNKS
    bounds, cuts = 0, []
    for i in range(chunks):
        cuts.append((i * tokens // chunks, (i + 1) * tokens // chunks))
    order = jnp.concatenate([got[:, :, a:b].reshape(2, -1) for a, b in cuts], axis=1)
    slot_id, scale = order[0].astype(jnp.int32), order[1]

    def to_dp(j):
        pairs = []
        for src in range(n_dp):
            for core in range(cores):
                q = core * per_core + (src % per_core + j) % per_core
                u = (src // per_core - core) % cores
                pairs.append((src * cores + core, q * cores + u))
        return pairs

    def to_group(u_of, j):
        pairs = []
        for q in range(n_dp):
            for core in range(cores):
                d1 = u_of(core)
                dest = ((q // per_core + d1) % cores) * per_core + (q % per_core - j) % per_core
                pairs.append((q * cores + core, dest * cores + core))
        return pairs

    gate_pre = saved_gate.astype(jnp.float32)
    up_pre = saved_up.astype(jnp.float32)
    sigmoid_gate = jax.nn.sigmoid(gate_pre)
    silu_gate = gate_pre * sigmoid_gate
    activation = (silu_gate * up_pre).astype(jnp.bfloat16)
    for_gate = up_pre * sigmoid_gate * (1.0 + gate_pre * (1.0 - sigmoid_gate))
    pick = (lax.broadcasted_iota(jnp.int32, (slot_count, slot_id.shape[0]), 0) == slot_id[None, :]).astype(
        jnp.bfloat16
    )
    in_tokens = lax.dot_general(
        pick, activation, (((0,), (0,)), ((), ())), preferred_element_type=jnp.float32
    )
    in_tokens = (in_tokens * scale[:, None]).astype(jnp.bfloat16)

    def from_group(u_of, j):
        return [(b, a) for a, b in to_group(u_of, j)]

    others = []
    for x in range(1, cores + 1):
        for j in range(per_core):
            u_of = lambda core, x=x: (core + x) % cores
            others.append(lax.ppermute(in_tokens, ("dp", "tensor"), from_group(u_of, j)))

    mine_x, other_x, partial = [], [], []
    for a, b in cuts:
        first = []
        for j in range(per_core):
            block = lax.dynamic_slice(
                out_grad, (jnp.int32(a), (p % per_core + j) % per_core * depth), (b - a, depth)
            )
            first.append(lax.ppermute(block, ("dp", "tensor"), to_dp(j)))
        first = jnp.stack(first)
        rows = jnp.stack([first] + [lax.ppermute(first, "expert", turn(k)) for k in range(1, owners)], axis=1)
        rows = rows.reshape(per_core, -1, depth)
        mine_x.append(rows)
        swapped = [
            lax.ppermute(rows, "tensor", [(c, (c - x) % cores) for c in range(cores)]) for x in range(1, cores)
        ]
        other_x.append(swapped)
        sums = None
        for x in range(cores):
            held = rows if x == 0 else swapped[x - 1]
            for j in range(per_core):
                piece = jnp.dot(held[j], weight, preferred_element_type=jnp.float32)
                piece = piece.astype(jnp.bfloat16)
                u_of = lambda core, x=x: (core + x) % cores
                piece = lax.ppermute(piece, ("dp", "tensor"), to_group(u_of, j)).astype(jnp.float32)
                sums = piece if sums is None else sums + piece
        partial.append(sums)

    total = jnp.concatenate(partial, axis=0) * scale[:, None]
    amax = jnp.max(jnp.abs(total)).reshape(1, 1)
    grad_amax = lax.pmax(amax, "tensor")
    high = total.astype(jnp.bfloat16)
    low = (total - high.astype(jnp.float32)).astype(jnp.bfloat16)
    grad_hidden = jnp.dot(pick, high, preferred_element_type=jnp.float32) + jnp.dot(
        pick, low, preferred_element_type=jnp.float32
    )
    quantized = (grad_hidden / (grad_amax + epsilon)).astype(jnp.bfloat16).astype(jnp.float32)
    grad_gate = (quantized * for_gate).astype(jnp.bfloat16)
    grad_up = (quantized * silu_gate).astype(jnp.bfloat16)

    weight_sum = 0.0
    for x in range(cores):
        for j in range(per_core):
            acts = others[(x - 1) % cores * per_core + j]
            held = jnp.concatenate(
                [(mine_x[i] if x == 0 else other_x[i][x - 1])[j] for i in range(chunks)], axis=0
            )
            weight_sum += lax.dot_general(
                held, acts, (((0,), (0,)), ((), ())), preferred_element_type=jnp.float32
            )
    return (weight_sum.astype(jnp.bfloat16).reshape(w_down.shape), grad_gate, grad_up, grad_amax)


CHUNKS = 2


def solution(mesh):
    placed = (
        P(("dp", "expert"), "tensor"),
        P(("dp", "expert"), None),
        P(("dp", "expert"), None),
        P("expert", "dp", "tensor"),
        P(("dp", "expert"), "tensor"),
        P(("dp", "expert"), "tensor"),
    )

    def body(out_grad, routing, route_probs, w_down, saved_gate, saved_up):
        capacity = saved_gate.shape[0] // mesh.shape["expert"]
        whole = capacity >= routing.shape[0] and mesh.shape["dp"] % mesh.shape["tensor"] == 0
        return (by_tokens if whole else by_slots)(
            out_grad, routing, route_probs, w_down, saved_gate, saved_up
        )

    return jax.shard_map(
        body,
        mesh=mesh,
        in_specs=placed,
        out_specs=(
            P("expert", "dp", "tensor"),
            P(("dp", "expert"), "tensor"),
            P(("dp", "expert"), "tensor"),
            P("dp", "expert"),
        ),
        check_vma=False,
    )
```

time: 172 us -> 103 us (0.60)
  waiting for transfers between devices: 119 us -> 35.7 us
  starting transfers between devices: 6.41 us -> 46.2 us
  between operations: 14.7 us -> 1.69 us
  other arithmetic: 9.81 us -> 2.99 us
  blocking collectives: 5.83 us -> 3.08 us
  local copies, waits for them, and re-layouts: 4.33 us -> 1.68 us
    all_to_all x1 -> x0, waiting for transfers between devices: 81.6 us -> none  [body(): lax.all_to_all((picked_rows.astype(jnp.float32) * slot_scale[:, :, None])...]
    ppermute x0 -> x27, starting transfers between devices: none -> 46.2 us  [the longest x4 12.9 us: by_tokens(): lax.ppermute(in_tokens, ('dp', 'tensor'), from_group(u_of, j))]
    reduce_scatter x1 -> x0, waiting for transfers between devices: 36.4 us -> none  [body(): lax.psum_scatter(lax.dot_general(columns, activation, (((0,), (0,)), ((),...]
    ppermute x0 -> x27, waiting for transfers between devices: none -> 35.7 us  [the longest x6 23.4 us: by_tokens(): lax.ppermute(first, 'expert', turn(k))]
    convert_element_type x3 -> x1, other arithmetic: 7.66 us -> 0.01 us  [by_tokens(): slot_id, scale = (order[0].astype(jnp.int32), order[1])]
    all_to_all x1 -> x0, starting transfers between devices: 6.37 us -> none  [body(): lax.all_to_all((picked_rows.astype(jnp.float32) * slot_scale[:, :, None])...]
    gather x1 -> x0, local copies, waits for them, and re-layouts: 4.15 us -> none  [body(): picked_rows = jnp.take(features, slot_token, axis=0)]
    all_gather x1 -> x0, blocking collectives: 2.75 us -> none  [body(): features = lax.all_gather(out_grad, 'tensor', axis=1, tiled=True)]
  transfers between devices with their start and end apart: 3 -> 27, of which waited for: 2 -> 8; matrix products, arithmetic and copies ran while one was open for 8% -> 10% of each run, Pallas kernels for 0% -> 0%
where the time goes in v1:
time: 103 us
  starting transfers between devices  46.2 us (45%)
  waiting for transfers between devices  35.7 us (35%)
  matrix products  11.4 us (11%)
  blocking collectives  3.08 us (3%)
  other arithmetic  2.99 us (3%)
  between operations  1.69 us (2%)
  local copies, waits for them, and re-layouts  1.68 us (2%)
    ppermute x6, waiting for transfers between devices, by_tokens(): lax.ppermute(first, 'expert', turn(k))  23.4 us
    ppermute x4, starting transfers between devices, by_tokens(): lax.ppermute(in_tokens, ('dp', 'tensor'), from_group(u_of, j))  12.9 us
    ppermute x8, starting transfers between devices, by_tokens(): lax.ppermute(piece, ('dp', 'tensor'), to_group(u_of, j)).astype(jnp.float32)  12.4 us
    ppermute x8, waiting for transfers between devices, by_tokens(): lax.ppermute(piece, ('dp', 'tensor'), to_group(u_of, j)).astype(jnp.float32)  10.5 us
    ppermute x3, starting transfers between devices, by_tokens(): lax.ppermute(lax.dynamic_index_in_dim(tables, (e + k) % owners, 0, keepdi...  7.01 us
    ppermute x6, starting transfers between devices, by_tokens(): lax.ppermute(first, 'expert', turn(k))  6.34 us
    ppermute x2, starting transfers between devices, by_tokens(): lax.ppermute(rows, 'tensor', [(c, (c - x) % cores) for c in range(cores)])  4.1 us
    dot_general x4, matrix products, by_tokens(): lax.dot_general(held, acts, (((0,), (0,)), ((), ())), preferred_element_t...  3.62 us
  transfers between devices with their start and end apart: 27, of which 8 were waited for; matrix products, arithmetic and copies ran while one was open for 10% of the time, Pallas kernels for 0%

profile of v1, /device:TPU:0, one launch (start us, length us, event | category | flops | bytes accessed | tf_op | source)
XLA Modules:
  0.0 102.7 jit_solution(494121480678464954)
XLA Ops:
  0.7 0.8 fusion.51
  1.5 0.7 select_reduce_fusion
  2.3 0.1 fusion.6
  2.5 3.1 %collective-permute-start.10 = (f32[2,128]{1,0:T(2,128)S(1)}, f32[2,128]{1,0:T(2,128)S(1)}, u32[]{:S(2)}, u32[]{:S(2)}) collective-permute-start(f32[2,128]{1,0:T(2,128)S(1)} %bitcast.121), channel_id=1, source_target_pairs={{0,2},{2,4},{4,6},{6,0},{1,3},{3,5},{5,7},{7,1},{8,10},{10,12},{12... | collective-permute-start | bytes 3080 | tf_op jit(solution)/shard_map/ppermute | solution.py:92
  5.5 2.6 %collective-permute-start.11 = (f32[2,128]{1,0:T(2,128)S(1)}, f32[2,128]{1,0:T(2,128)S(1)}, u32[]{:S(2)}, u32[]{:S(2)}) collective-permute-start(f32[2,128]{1,0:T(2,128)S(1)} %bitcast.120), channel_id=1, source_target_pairs={{0,4},{2,6},{4,0},{6,2},{1,5},{3,7},{5,1},{7,3},{8,12},{10,14},{12... | collective-permute-start | bytes 3080 | tf_op jit(solution)/shard_map/ppermute | solution.py:92
  8.1 1.3 %collective-permute-start.12 = (f32[2,128]{1,0:T(2,128)S(1)}, f32[2,128]{1,0:T(2,128)S(1)}, u32[]{:S(2)}, u32[]{:S(2)}) collective-permute-start(f32[2,128]{1,0:T(2,128)S(1)} %bitcast.119), channel_id=1, source_target_pairs={{0,6},{2,0},{4,2},{6,4},{1,7},{3,1},{5,3},{7,5},{8,14},{10,8},{12,... | collective-permute-start | bytes 3080 | tf_op jit(solution)/shard_map/ppermute | solution.py:92
  9.5 1.1 %constant_dynamic-slice_fusion.1 = (bf16[64,896]{1,0:T(8,128)(2,1)S(1)}, bf16[64,896]{1,0:T(8,128)(2,1)S(1)}, bf16[64,896]{1,0:T(8,128)(2,1)S(1)}, bf16[64,896]{1,0:T(8,128)(2,1)S(1)}) fusion(bf16[128,1792]{1,0:T(8,128)(2,1)} %param.6, s32[]{:T(128)S(6)} %select_n.69, s32[]{:T(128)S(6)} %select_n.71), kind=kLoop, calls=%fused_computation.96 | loop fusion | bytes 917512 | tf_op jit(solution)/shard_map/dynamic_slice | solution.py:151
  10.6 0.7 collective-permute-start
  11.2 1.5 %collective-permute-start.1 = (bf16[64,896]{1,0:T(8,128)(2,1)S(1)}, bf16[64,896]{1,0:T(8,128)(2,1)S(1)}, u32[]{:S(2)}, u32[]{:S(2)}) collective-permute-start(bf16[64,896]{1,0:T(8,128)(2,1)S(1)} %get-tuple-element.15), channel_id=1, source_target_pairs={{0,8},{1,25},{8,0},{9,17},{16,9},{17,24},{24,1},{25,16},{2,10},{3,... | collective-permute-start | bytes 344072 | tf_op jit(solution)/shard_map/ppermute | solution.py:154
  12.8 0.7 collective-permute-start.5
  13.5 0.6 collective-permute-start.6
  14.2 0.1 reshape.38
  14.2 0.1 reshape.39
  14.4 1.7 %collective-permute-done.1 = bf16[64,896]{1,0:T(8,128)(2,1)S(1)} collective-permute-done((bf16[64,896]{1,0:T(8,128)(2,1)S(1)}, bf16[64,896]{1,0:T(8,128)(2,1)S(1)}, u32[]{:S(2)}, u32[]{:S(2)}) %collective-permute-start.1) | collective-permute-done | bytes 114720 | tf_op jit(solution)/shard_map/ppermute | solution.py:154
  16.1 0.7 collective-permute-start.2
  16.9 0.3 collective-permute-start.3
  17.2 2.8 %collective-permute-start.4 = (bf16[2,64,896]{2,1,0:T(8,128)(2,1)S(1)}, bf16[2,64,896]{2,1,0:T(8,128)(2,1)S(1)}, u32[]{:S(2)}, u32[]{:S(2)}) collective-permute-start(bf16[2,64,896]{2,1,0:T(8,128)(2,1)S(1)} %get-tuple-element.19), channel_id=1, source_target_pairs={{0,6},{2,0},{4,2},{6,4},{1,7},{3,1},{5,3},{7,5},{8,14},{10,8},{12,... | collective-permute-start | bytes 688136 | tf_op jit(solution)/shard_map/ppermute | solution.py:156
  20.0 0.7 fusion.2
  20.7 1.6 %collective-permute-start.14 = (bf16[512,512]{1,0:T(8,128)(2,1)S(1)}, bf16[512,512]{1,0:T(8,128)(2,1)S(1)}, u32[]{:S(2)}, u32[]{:S(2)}) collective-permute-start(bf16[512,512]{1,0:T(8,128)(2,1)S(1)} %fusion.2), channel_id=1, source_target_pairs={{8,0},{25,1},{0,8},{17,9},{24,16},{9,17},{16,24},{1,25},{10,2},{27... | collective-permute-start | bytes 1572872 | tf_op jit(solution)/shard_map/ppermute | solution.py:145
  22.3 0.7 collective-permute-start.13
  23.0 1.9 %collective-permute-done.2 = bf16[2,64,896]{2,1,0:T(8,128)(2,1)S(1)} collective-permute-done((bf16[2,64,896]{2,1,0:T(8,128)(2,1)S(1)}, bf16[2,64,896]{2,1,0:T(8,128)(2,1)S(1)}, u32[]{:S(2)}, u32[]{:S(2)}) %collective-permute-start.2) | collective-permute-done | bytes 229408 | tf_op jit(solution)/shard_map/ppermute | solution.py:156
  24.9 12.0 %collective-permute-done.3 = bf16[2,64,896]{2,1,0:T(8,128)(2,1)S(1)} collective-permute-done((bf16[2,64,896]{2,1,0:T(8,128)(2,1)S(1)}, bf16[2,64,896]{2,1,0:T(8,128)(2,1)S(1)}, u32[]{:S(2)}, u32[]{:S(2)}) %collective-permute-start.3) | collective-permute-done | bytes 229408 | tf_op jit(solution)/shard_map/ppermute | solution.py:156
  36.9 2.5 %collective-permute-start.9 = (bf16[2,64,896]{2,1,0:T(8,128)(2,1)S(1)}, bf16[2,64,896]{2,1,0:T(8,128)(2,1)S(1)}, u32[]{:S(2)}, u32[]{:S(2)}) collective-permute-start(bf16[2,64,896]{2,1,0:T(8,128)(2,1)S(1)} %get-tuple-element.21), channel_id=1, source_target_pairs={{0,6},{2,0},{4,2},{6,4},{1,7},{3,1},{5,3},{7,5},{8,14},{10,8},{12,... | collective-permute-start | bytes 688136 | tf_op jit(solution)/shard_map/ppermute | solution.py:156
  39.4 0.1 pad_maximum_fusion
  39.5 0.1 fusion.66
  39.6 0.4 convolution_convert_fusion.7
  40.1 0.4 convolution_convert_fusion.6
  40.5 6.4 %collective-permute-start.17 = (bf16[512,512]{1,0:T(8,128)(2,1)S(1)}, bf16[512,512]{1,0:T(8,128)(2,1)S(1)}, u32[]{:S(2)}, u32[]{:S(2)}) collective-permute-start(bf16[512,512]{1,0:T(8,128)(2,1)S(1)} %fusion.2), channel_id=1, source_target_pairs={{16,0},{1,1},{24,8},{9,9},{0,16},{17,17},{8,24},{25,25},{18,2},{3,... | collective-permute-start | bytes 1572872 | tf_op jit(solution)/shard_map/ppermute | solution.py:145
  46.9 8.6 %collective-permute-done.8 = bf16[2,64,896]{2,1,0:T(8,128)(2,1)S(1)} collective-permute-done((bf16[2,64,896]{2,1,0:T(8,128)(2,1)S(1)}, bf16[2,64,896]{2,1,0:T(8,128)(2,1)S(1)}, u32[]{:S(2)}, u32[]{:S(2)}) %collective-permute-start.8) | collective-permute-done | bytes 229408 | tf_op jit(solution)/shard_map/ppermute | solution.py:156
  55.6 4.3 %collective-permute-start.18 = (bf16[512,512]{1,0:T(8,128)(2,1)S(1)}, bf16[512,512]{1,0:T(8,128)(2,1)S(1)}, u32[]{:S(2)}, u32[]{:S(2)}) collective-permute-start(bf16[512,512]{1,0:T(8,128)(2,1)S(1)} %fusion.2), channel_id=1, source_target_pairs={{24,0},{9,1},{16,8},{1,9},{8,16},{25,17},{0,24},{17,25},{26,2},{11... | collective-permute-start | bytes 1572872 | tf_op jit(solution)/shard_map/ppermute | solution.py:145
  59.9 0.8 collective-permute-done.9
  60.7 0.1 collective-permute-start.15
  60.8 0.1 pad_maximum_fusion.1
  60.9 0.1 fusion.67
  61.0 0.4 convolution_convert_fusion.3
  61.5 0.4 convolution_convert_fusion.2
  61.9 0.7 collective-permute-start.19
  62.6 0.7 fusion.21
  63.3 4.0 %collective-permute-start.16 = (bf16[2,256,896]{2,1,0:T(8,128)(2,1)S(1)}, bf16[2,256,896]{2,1,0:T(8,128)(2,1)S(1)}, u32[]{:S(2)}, u32[]{:S(2)}) collective-permute-start(bf16[2,256,896]{2,1,0:T(8,128)(2,1)S(1)} %bitcast.92), channel_id=1, source_target_pairs={{0,1},{1,0},{2,3},{3,2},{4,5},{5,4},{6,7},{7,6},{8,9},{9,8},{10,11... | collective-permute-start | bytes 2752520 | tf_op jit(solution)/shard_map/ppermute | solution.py:160
  67.3 0.7 fusion.17
  68.0 1.6 %collective-permute-start.20 = (bf16[256,512]{1,0:T(8,128)(2,1)S(1)}, bf16[256,512]{1,0:T(8,128)(2,1)S(1)}, u32[]{:S(2)}, u32[]{:S(2)}) collective-permute-start(bf16[256,512]{1,0:T(8,128)(2,1)S(1)} %convolution_convert_fusion.6), channel_id=1, source_target_pairs={{0,8},{1,25},{8,0},{9,17},{16,24},{17,9},{24,16},{25,1},{2,10},{3,... | collective-permute-start | bytes 786440 | tf_op jit(solution)/shard_map/ppermute | solution.py:170
  69.6 0.1 slice_bitcast_fusion.1
  69.7 0.4 convolution_convert_fusion.5
  70.1 0.4 convolution_convert_fusion.4
  70.6 0.7 collective-permute-start.23
  71.3 0.4 convolution_convert_fusion.1
  71.7 0.1 slice_bitcast_fusion
  71.8 2.2 %collective-permute-start.21 = (bf16[256,512]{1,0:T(8,128)(2,1)S(1)}, bf16[256,512]{1,0:T(8,128)(2,1)S(1)}, u32[]{:S(2)}, u32[]{:S(2)}) collective-permute-start(bf16[256,512]{1,0:T(8,128)(2,1)S(1)} %convolution_convert_fusion.5), channel_id=1, source_target_pairs={{0,16},{1,1},{8,24},{9,9},{16,0},{17,17},{24,8},{25,25},{2,18},{3,... | collective-permute-start | bytes 786440 | tf_op jit(solution)/shard_map/ppermute | solution.py:170
  74.0 0.7 fusion.25
  74.7 1.7 %collective-permute-start.22 = (bf16[256,512]{1,0:T(8,128)(2,1)S(1)}, bf16[256,512]{1,0:T(8,128)(2,1)S(1)}, u32[]{:S(2)}, u32[]{:S(2)}) collective-permute-start(bf16[256,512]{1,0:T(8,128)(2,1)S(1)} %convolution_convert_fusion.4), channel_id=1, source_target_pairs={{0,24},{1,9},{8,16},{9,1},{16,8},{17,25},{24,0},{25,17},{2,26},{3,... | collective-permute-start | bytes 786440 | tf_op jit(solution)/shard_map/ppermute | solution.py:170
  76.4 1.6 %fusion.16 = bf16[1,896,512]{2,1,0:T(8,128)(2,1)} fusion(f32[896,512]{1,0:T(8,128)S(1)} %fusion.25, f32[896,512]{1,0:T(8,128)S(1)} %fusion.17, f32[896,512]{1,0:T(8,128)S(1)} %fusion.21, bf16[512,512]{1,0:T(8,128)(2,1)S(1)} %collective-permute-done.18, bf16[256,896]{1,0:T(8,128)(2,1)S(1)} %get-tuple-element.8, bf16[256,896]{1,0:T(8,128)(2,1)S(1)} %get-tuple-element.6), kind=kOutput, calls=%fused_computation.39 | convolution fusion | flops 473432064 | bytes 7864320 | tf_op jit(solution)/shard_map/dot_general | solution.py:193
  78.0 0.4 convolution_convert_fusion
  78.4 1.6 %collective-permute-start.24 = (bf16[256,512]{1,0:T(8,128)(2,1)S(1)}, bf16[256,512]{1,0:T(8,128)(2,1)S(1)}, u32[]{:S(2)}, u32[]{:S(2)}) collective-permute-start(bf16[256,512]{1,0:T(8,128)(2,1)S(1)} %convolution_convert_fusion.2), channel_id=1, source_target_pairs={{0,8},{1,25},{8,0},{9,17},{16,24},{17,9},{24,16},{25,1},{2,10},{3,... | collective-permute-start | bytes 786440 | tf_op jit(solution)/shard_map/ppermute | solution.py:170
  80.1 2.2 %collective-permute-start.25 = (bf16[256,512]{1,0:T(8,128)(2,1)S(1)}, bf16[256,512]{1,0:T(8,128)(2,1)S(1)}, u32[]{:S(2)}, u32[]{:S(2)}) collective-permute-start(bf16[256,512]{1,0:T(8,128)(2,1)S(1)} %convolution_convert_fusion.1), channel_id=1, source_target_pairs={{0,16},{1,1},{8,24},{9,9},{16,0},{17,17},{24,8},{25,25},{2,18},{3,... | collective-permute-start | bytes 786440 | tf_op jit(solution)/shard_map/ppermute | solution.py:170
  82.2 4.5 %collective-permute-done.21 = bf16[256,512]{1,0:T(8,128)(2,1)S(1)} collective-permute-done((bf16[256,512]{1,0:T(8,128)(2,1)S(1)}, bf16[256,512]{1,0:T(8,128)(2,1)S(1)}, u32[]{:S(2)}, u32[]{:S(2)}) %collective-permute-start.21) | collective-permute-done | bytes 262176 | tf_op jit(solution)/shard_map/ppermute | solution.py:170
  86.7 1.7 %collective-permute-start.26 = (bf16[256,512]{1,0:T(8,128)(2,1)S(1)}, bf16[256,512]{1,0:T(8,128)(2,1)S(1)}, u32[]{:S(2)}, u32[]{:S(2)}) collective-permute-start(bf16[256,512]{1,0:T(8,128)(2,1)S(1)} %convolution_convert_fusion), channel_id=1, source_target_pairs={{0,24},{1,9},{8,16},{9,1},{16,8},{17,25},{24,0},{25,17},{2,26},{3,... | collective-permute-start | bytes 786440 | tf_op jit(solution)/shard_map/ppermute | solution.py:170
  88.4 0.1 convert_add_fusion.1
  88.6 2.3 %collective-permute-done.24 = bf16[256,512]{1,0:T(8,128)(2,1)S(1)} collective-permute-done((bf16[256,512]{1,0:T(8,128)(2,1)S(1)}, bf16[256,512]{1,0:T(8,128)(2,1)S(1)}, u32[]{:S(2)}, u32[]{:S(2)}) %collective-permute-start.24) | collective-permute-done | bytes 262176 | tf_op jit(solution)/shard_map/ppermute | solution.py:170
  90.8 3.8 %collective-permute-done.26 = bf16[256,512]{1,0:T(8,128)(2,1)S(1)} collective-permute-done((bf16[256,512]{1,0:T(8,128)(2,1)S(1)}, bf16[256,512]{1,0:T(8,128)(2,1)S(1)}, u32[]{:S(2)}, u32[]{:S(2)}) %collective-permute-start.26) | collective-permute-done | bytes 262176 | tf_op jit(solution)/shard_map/ppermute | solution.py:170
  94.6 0.1 convert_add_fusion
  94.7 0.5 fusion.15
  95.2 0.8 abs_reduce_fusion
  96.0 3.1 %pmax.7 = f32[1,1]{1,0:T(1,128)} all-reduce(f32[1,1]{1,0:T(1,128)} %bitcast.43), channel_id=1, replica_groups=mesh['dp'=4,'expert'=4,'tensor'=2] {'tensor'}, use_global_device_ids=true, to_apply=%region_3.4 | all-reduce | flops 1 | bytes 8 | tf_op jit(solution)/shard_map/pmax | solution.py:176
  99.8 3.0 %fusion.10 = (bf16[512,512]{1,0:T(8,128)(2,1)}, bf16[512,512]{1,0:T(8,128)(2,1)}) fusion(bf16[512,512]{1,0:T(8,128)(2,1)} %param.10, bf16[512,512]{1,0:T(8,128)(2,1)S(1)} %copy-done.1, f32[]{:T(128)} %bitcast.44, f32[512,512]{1,0:T(8,128)S(1)} %fusion.15, f32[256,512]{1,0:T(8,128)S(1)} %convert_add_fusion, f32[256,512]{1,0:T(8,128)S(1)} %convert_add_fusion.1, ...), kind=kOutput, calls=%fused_computation.29 | convolution fusion | flops 275251200 | bytes 4198404 | tf_op jit(solution)/shard_map/dot_general | solution.py:179
  (35 shorter events, 0.3 us)
Async XLA Ops:
  0.6 39.0 %copy-start = (bf16[1,896,512]{2,1,0:T(8,128)(2,1)S(1)}, bf16[1,896,512]{2,1,0:T(8,128)(2,1)}, u32[]{:S(2)}) copy-start(bf16[1,896,512]{2,1,0:T(8,128)(2,1)} %param.9) | copy-start | bytes 2752516
  0.6 19.4 %copy-start.2 = (bf16[512,512]{1,0:T(8,128)(2,1)S(1)}, bf16[512,512]{1,0:T(8,128)(2,1)}, u32[]{:S(2)}) copy-start(bf16[512,512]{1,0:T(8,128)(2,1)} %param.10) | copy-start | bytes 1572868
  0.7 19.4 %copy-start.1 = (bf16[512,512]{1,0:T(8,128)(2,1)S(1)}, bf16[512,512]{1,0:T(8,128)(2,1)}, u32[]{:S(2)}) copy-start(bf16[512,512]{1,0:T(8,128)(2,1)} %param.11) | copy-start | bytes 1572868
  2.5 10.3 %collective-permute-start.10 = (f32[2,128]{1,0:T(2,128)S(1)}, f32[2,128]{1,0:T(2,128)S(1)}, u32[]{:S(2)}, u32[]{:S(2)}) collective-permute-start(f32[2,128]{1,0:T(2,128)S(1)} %bitcast.121), channel_id=1, source_target_pairs={{0,2},{2,4},{4,6},{6,0},{1,3},{3,5},{5,7},{7,1},{8,10},{10,12},{12... | collective-permute-start | bytes 3080 | tf_op jit(solution)/shard_map/ppermute | solution.py:92
  5.5 7.9 %collective-permute-start.11 = (f32[2,128]{1,0:T(2,128)S(1)}, f32[2,128]{1,0:T(2,128)S(1)}, u32[]{:S(2)}, u32[]{:S(2)}) collective-permute-start(f32[2,128]{1,0:T(2,128)S(1)} %bitcast.120), channel_id=1, source_target_pairs={{0,4},{2,6},{4,0},{6,2},{1,5},{3,7},{5,1},{7,3},{8,12},{10,14},{12... | collective-permute-start | bytes 3080 | tf_op jit(solution)/shard_map/ppermute | solution.py:92
  8.1 5.9 %collective-permute-start.12 = (f32[2,128]{1,0:T(2,128)S(1)}, f32[2,128]{1,0:T(2,128)S(1)}, u32[]{:S(2)}, u32[]{:S(2)}) collective-permute-start(f32[2,128]{1,0:T(2,128)S(1)} %bitcast.119), channel_id=1, source_target_pairs={{0,6},{2,0},{4,2},{6,4},{1,7},{3,1},{5,3},{7,5},{8,14},{10,8},{12,... | collective-permute-start | bytes 3080 | tf_op jit(solution)/shard_map/ppermute | solution.py:92
  10.6 3.8 %collective-permute-start = (bf16[64,896]{1,0:T(8,128)(2,1)S(1)}, bf16[64,896]{1,0:T(8,128)(2,1)S(1)}, u32[]{:S(2)}, u32[]{:S(2)}) collective-permute-start(bf16[64,896]{1,0:T(8,128)(2,1)S(1)} %get-tuple-element.14), channel_id=1, source_target_pairs={{0,0},{1,17},{8,8},{9,25},{16,1},{17,16},{24,9},{25,24},{2,2},{3,1... | collective-permute-start | bytes 344072 | tf_op jit(solution)/shard_map/ppermute | solution.py:154
  11.2 4.8 %collective-permute-start.1 = (bf16[64,896]{1,0:T(8,128)(2,1)S(1)}, bf16[64,896]{1,0:T(8,128)(2,1)S(1)}, u32[]{:S(2)}, u32[]{:S(2)}) collective-permute-start(bf16[64,896]{1,0:T(8,128)(2,1)S(1)} %get-tuple-element.15), channel_id=1, source_target_pairs={{0,8},{1,25},{8,0},{9,17},{16,9},{17,24},{24,1},{25,16},{2,10},{3,... | collective-permute-start | bytes 344072 | tf_op jit(solution)/shard_map/ppermute | solution.py:154
  12.8 7.9 %collective-permute-start.5 = (bf16[64,896]{1,0:T(8,128)(2,1)S(1)}, bf16[64,896]{1,0:T(8,128)(2,1)S(1)}, u32[]{:S(2)}, u32[]{:S(2)}) collective-permute-start(bf16[64,896]{1,0:T(8,128)(2,1)S(1)} %get-tuple-element.17), channel_id=1, source_target_pairs={{0,0},{1,17},{8,8},{9,25},{16,1},{17,16},{24,9},{25,24},{2,2},{3,1... | collective-permute-start | bytes 344072 | tf_op jit(solution)/shard_map/ppermute | solution.py:154
  13.5 8.8 %collective-permute-start.6 = (bf16[64,896]{1,0:T(8,128)(2,1)S(1)}, bf16[64,896]{1,0:T(8,128)(2,1)S(1)}, u32[]{:S(2)}, u32[]{:S(2)}) collective-permute-start(bf16[64,896]{1,0:T(8,128)(2,1)S(1)} %get-tuple-element.16), channel_id=1, source_target_pairs={{0,8},{1,25},{8,0},{9,17},{16,9},{17,24},{24,1},{25,16},{2,10},{3,... | collective-permute-start | bytes 344072 | tf_op jit(solution)/shard_map/ppermute | solution.py:154
  16.1 8.8 %collective-permute-start.2 = (bf16[2,64,896]{2,1,0:T(8,128)(2,1)S(1)}, bf16[2,64,896]{2,1,0:T(8,128)(2,1)S(1)}, u32[]{:S(2)}, u32[]{:S(2)}) collective-permute-start(bf16[2,64,896]{2,1,0:T(8,128)(2,1)S(1)} %get-tuple-element.19), channel_id=1, source_target_pairs={{0,2},{2,4},{4,6},{6,0},{1,3},{3,5},{5,7},{7,1},{8,10},{10,12},{12... | collective-permute-start | bytes 688136 | tf_op jit(solution)/shard_map/ppermute | solution.py:156
  16.9 20.1 %collective-permute-start.3 = (bf16[2,64,896]{2,1,0:T(8,128)(2,1)S(1)}, bf16[2,64,896]{2,1,0:T(8,128)(2,1)S(1)}, u32[]{:S(2)}, u32[]{:S(2)}) collective-permute-start(bf16[2,64,896]{2,1,0:T(8,128)(2,1)S(1)} %get-tuple-element.19), channel_id=1, source_target_pairs={{0,4},{2,6},{4,0},{6,2},{1,5},{3,7},{5,1},{7,3},{8,12},{10,14},{12... | collective-permute-start | bytes 688136 | tf_op jit(solution)/shard_map/ppermute | solution.py:156
  17.2 19.7 %collective-permute-start.4 = (bf16[2,64,896]{2,1,0:T(8,128)(2,1)S(1)}, bf16[2,64,896]{2,1,0:T(8,128)(2,1)S(1)}, u32[]{:S(2)}, u32[]{:S(2)}) collective-permute-start(bf16[2,64,896]{2,1,0:T(8,128)(2,1)S(1)} %get-tuple-element.19), channel_id=1, source_target_pairs={{0,6},{2,0},{4,2},{6,4},{1,7},{3,1},{5,3},{7,5},{8,14},{10,8},{12,... | collective-permute-start | bytes 688136 | tf_op jit(solution)/shard_map/ppermute | solution.py:156
  20.7 41.2 %collective-permute-start.14 = (bf16[512,512]{1,0:T(8,128)(2,1)S(1)}, bf16[512,512]{1,0:T(8,128)(2,1)S(1)}, u32[]{:S(2)}, u32[]{:S(2)}) collective-permute-start(bf16[512,512]{1,0:T(8,128)(2,1)S(1)} %fusion.2), channel_id=1, source_target_pairs={{8,0},{25,1},{0,8},{17,9},{24,16},{9,17},{16,24},{1,25},{10,2},{27... | collective-permute-start | bytes 1572872 | tf_op jit(solution)/shard_map/ppermute | solution.py:145
  22.3 41.0 %collective-permute-start.13 = (bf16[512,512]{1,0:T(8,128)(2,1)S(1)}, bf16[512,512]{1,0:T(8,128)(2,1)S(1)}, u32[]{:S(2)}, u32[]{:S(2)}) collective-permute-start(bf16[512,512]{1,0:T(8,128)(2,1)S(1)} %fusion.2), channel_id=1, source_target_pairs={{0,0},{17,1},{8,8},{25,9},{16,16},{1,17},{24,24},{9,25},{2,2},{19,... | collective-permute-start | bytes 1572872 | tf_op jit(solution)/shard_map/ppermute | solution.py:145
  24.9 15.6 %collective-permute-start.7 = (bf16[2,64,896]{2,1,0:T(8,128)(2,1)S(1)}, bf16[2,64,896]{2,1,0:T(8,128)(2,1)S(1)}, u32[]{:S(2)}, u32[]{:S(2)}) collective-permute-start(bf16[2,64,896]{2,1,0:T(8,128)(2,1)S(1)} %get-tuple-element.21), channel_id=1, source_target_pairs={{0,2},{2,4},{4,6},{6,0},{1,3},{3,5},{5,7},{7,1},{8,10},{10,12},{12... | collective-permute-start | bytes 688136 | tf_op jit(solution)/shard_map/ppermute | solution.py:156
  36.9 18.6 %collective-permute-start.8 = (bf16[2,64,896]{2,1,0:T(8,128)(2,1)S(1)}, bf16[2,64,896]{2,1,0:T(8,128)(2,1)S(1)}, u32[]{:S(2)}, u32[]{:S(2)}) collective-permute-start(bf16[2,64,896]{2,1,0:T(8,128)(2,1)S(1)} %get-tuple-element.21), channel_id=1, source_target_pairs={{0,4},{2,6},{4,0},{6,2},{1,5},{3,7},{5,1},{7,3},{8,12},{10,14},{12... | collective-permute-start | bytes 688136 | tf_op jit(solution)/shard_map/ppermute | solution.py:156
  36.9 23.8 %collective-permute-start.9 = (bf16[2,64,896]{2,1,0:T(8,128)(2,1)S(1)}, bf16[2,64,896]{2,1,0:T(8,128)(2,1)S(1)}, u32[]{:S(2)}, u32[]{:S(2)}) collective-permute-start(bf16[2,64,896]{2,1,0:T(8,128)(2,1)S(1)} %get-tuple-element.21), channel_id=1, source_target_pairs={{0,6},{2,0},{4,2},{6,4},{1,7},{3,1},{5,3},{7,5},{8,14},{10,8},{12,... | collective-permute-start | bytes 688136 | tf_op jit(solution)/shard_map/ppermute | solution.py:156
  40.5 31.3 %collective-permute-start.17 = (bf16[512,512]{1,0:T(8,128)(2,1)S(1)}, bf16[512,512]{1,0:T(8,128)(2,1)S(1)}, u32[]{:S(2)}, u32[]{:S(2)}) collective-permute-start(bf16[512,512]{1,0:T(8,128)(2,1)S(1)} %fusion.2), channel_id=1, source_target_pairs={{16,0},{1,1},{24,8},{9,9},{0,16},{17,17},{8,24},{25,25},{18,2},{3,... | collective-permute-start | bytes 1572872 | tf_op jit(solution)/shard_map/ppermute | solution.py:145
  55.6 19.1 %collective-permute-start.18 = (bf16[512,512]{1,0:T(8,128)(2,1)S(1)}, bf16[512,512]{1,0:T(8,128)(2,1)S(1)}, u32[]{:S(2)}, u32[]{:S(2)}) collective-permute-start(bf16[512,512]{1,0:T(8,128)(2,1)S(1)} %fusion.2), channel_id=1, source_target_pairs={{24,0},{9,1},{16,8},{1,9},{8,16},{25,17},{0,24},{17,25},{26,2},{11... | collective-permute-start | bytes 1572872 | tf_op jit(solution)/shard_map/ppermute | solution.py:145
  60.7 7.3 %collective-permute-start.15 = (bf16[2,256,896]{2,1,0:T(8,128)(2,1)S(1)}, bf16[2,256,896]{2,1,0:T(8,128)(2,1)S(1)}, u32[]{:S(2)}, u32[]{:S(2)}) collective-permute-start(bf16[2,256,896]{2,1,0:T(8,128)(2,1)S(1)} %bitcast.91), channel_id=1, source_target_pairs={{0,1},{1,0},{2,3},{3,2},{4,5},{5,4},{6,7},{7,6},{8,9},{9,8},{10,11... | collective-permute-start | bytes 2752520 | tf_op jit(solution)/shard_map/ppermute | solution.py:160
  61.9 16.5 %collective-permute-start.19 = (bf16[256,512]{1,0:T(8,128)(2,1)S(1)}, bf16[256,512]{1,0:T(8,128)(2,1)S(1)}, u32[]{:S(2)}, u32[]{:S(2)}) collective-permute-start(bf16[256,512]{1,0:T(8,128)(2,1)S(1)} %convolution_convert_fusion.7), channel_id=1, source_target_pairs={{0,0},{1,17},{8,8},{9,25},{16,16},{17,1},{24,24},{25,9},{2,2},{3,1... | collective-permute-start | bytes 786440 | tf_op jit(solution)/shard_map/ppermute | solution.py:170
  63.3 7.3 %collective-permute-start.16 = (bf16[2,256,896]{2,1,0:T(8,128)(2,1)S(1)}, bf16[2,256,896]{2,1,0:T(8,128)(2,1)S(1)}, u32[]{:S(2)}, u32[]{:S(2)}) collective-permute-start(bf16[2,256,896]{2,1,0:T(8,128)(2,1)S(1)} %bitcast.92), channel_id=1, source_target_pairs={{0,1},{1,0},{2,3},{3,2},{4,5},{5,4},{6,7},{7,6},{8,9},{9,8},{10,11... | collective-permute-start | bytes 2752520 | tf_op jit(solution)/shard_map/ppermute | solution.py:160
  68.0 12.1 %collective-permute-start.20 = (bf16[256,512]{1,0:T(8,128)(2,1)S(1)}, bf16[256,512]{1,0:T(8,128)(2,1)S(1)}, u32[]{:S(2)}, u32[]{:S(2)}) collective-permute-start(bf16[256,512]{1,0:T(8,128)(2,1)S(1)} %convolution_convert_fusion.6), channel_id=1, source_target_pairs={{0,8},{1,25},{8,0},{9,17},{16,24},{17,9},{24,16},{25,1},{2,10},{3,... | collective-permute-start | bytes 786440 | tf_op jit(solution)/shard_map/ppermute | solution.py:170
  70.6 18.0 %collective-permute-start.23 = (bf16[256,512]{1,0:T(8,128)(2,1)S(1)}, bf16[256,512]{1,0:T(8,128)(2,1)S(1)}, u32[]{:S(2)}, u32[]{:S(2)}) collective-permute-start(bf16[256,512]{1,0:T(8,128)(2,1)S(1)} %convolution_convert_fusion.3), channel_id=1, source_target_pairs={{0,0},{1,17},{8,8},{9,25},{16,16},{17,1},{24,24},{25,9},{2,2},{3,1... | collective-permute-start | bytes 786440 | tf_op jit(solution)/shard_map/ppermute | solution.py:170
  71.8 15.0 %collective-permute-start.21 = (bf16[256,512]{1,0:T(8,128)(2,1)S(1)}, bf16[256,512]{1,0:T(8,128)(2,1)S(1)}, u32[]{:S(2)}, u32[]{:S(2)}) collective-permute-start(bf16[256,512]{1,0:T(8,128)(2,1)S(1)} %convolution_convert_fusion.5), channel_id=1, source_target_pairs={{0,16},{1,1},{8,24},{9,9},{16,0},{17,17},{24,8},{25,25},{2,18},{3,... | collective-permute-start | bytes 786440 | tf_op jit(solution)/shard_map/ppermute | solution.py:170
  74.7 13.7 %collective-permute-start.22 = (bf16[256,512]{1,0:T(8,128)(2,1)S(1)}, bf16[256,512]{1,0:T(8,128)(2,1)S(1)}, u32[]{:S(2)}, u32[]{:S(2)}) collective-permute-start(bf16[256,512]{1,0:T(8,128)(2,1)S(1)} %convolution_convert_fusion.4), channel_id=1, source_target_pairs={{0,24},{1,9},{8,16},{9,1},{16,8},{17,25},{24,0},{25,17},{2,26},{3,... | collective-permute-start | bytes 786440 | tf_op jit(solution)/shard_map/ppermute | solution.py:170
  78.4 12.4 %collective-permute-start.24 = (bf16[256,512]{1,0:T(8,128)(2,1)S(1)}, bf16[256,512]{1,0:T(8,128)(2,1)S(1)}, u32[]{:S(2)}, u32[]{:S(2)}) collective-permute-start(bf16[256,512]{1,0:T(8,128)(2,1)S(1)} %convolution_convert_fusion.2), channel_id=1, source_target_pairs={{0,8},{1,25},{8,0},{9,17},{16,24},{17,9},{24,16},{25,1},{2,10},{3,... | collective-permute-start | bytes 786440 | tf_op jit(solution)/shard_map/ppermute | solution.py:170
  80.1 10.8 %collective-permute-start.25 = (bf16[256,512]{1,0:T(8,128)(2,1)S(1)}, bf16[256,512]{1,0:T(8,128)(2,1)S(1)}, u32[]{:S(2)}, u32[]{:S(2)}) collective-permute-start(bf16[256,512]{1,0:T(8,128)(2,1)S(1)} %convolution_convert_fusion.1), channel_id=1, source_target_pairs={{0,16},{1,1},{8,24},{9,9},{16,0},{17,17},{24,8},{25,25},{2,18},{3,... | collective-permute-start | bytes 786440 | tf_op jit(solution)/shard_map/ppermute | solution.py:170
  86.7 7.9 %collective-permute-start.26 = (bf16[256,512]{1,0:T(8,128)(2,1)S(1)}, bf16[256,512]{1,0:T(8,128)(2,1)S(1)}, u32[]{:S(2)}, u32[]{:S(2)}) collective-permute-start(bf16[256,512]{1,0:T(8,128)(2,1)S(1)} %convolution_convert_fusion), channel_id=1, source_target_pairs={{0,24},{1,9},{8,16},{9,1},{16,8},{17,25},{24,0},{25,17},{2,26},{3,... | collective-permute-start | bytes 786440 | tf_op jit(solution)/shard_map/ppermute | solution.py:170

commit v2 on v1

--- a/solution.py
+++ b/solution.py
@@ -79,47 +79,64 @@
     depth, hidden = w_down.shape[1:]
     slot_count = saved_gate.shape[0]
     capacity = slot_count // owners
-    per_core = n_dp // cores
+    part = tokens // cores
     weight = w_down[0]
 
     def turn(k):
         return [(s, (s + k) % owners) for s in range(owners)]
+
+    def over_dp(x, d):
+        return lax.ppermute(x, "dp", [(q, q ^ d) for q in range(n_dp)])
+
+    def swap(x):
+        return lax.ppermute(x, "tensor", [(c, 1 - c) for c in range(cores)])
+
+    keep = lax.dynamic_slice_in_dim(out_grad, t * part, part, 0)
+    give = lax.dynamic_slice_in_dim(out_grad, (1 - t) * part, part, 0)
+    came = swap(give)
+    share = jnp.where(t == 0, jnp.concatenate([keep, came], axis=1), jnp.concatenate([came, keep], axis=1))
+    blocks = [lax.dynamic_slice(share, (jnp.int32(0), (p ^ d) * depth), (part, depth)) for d in range(n_dp)]
+    blocks = [over_dp(x, d) if d else x for d, x in enumerate(blocks)]
 
     is_routed, scaling, slot_rank = route(routing, route_probs, owners)
     slot_of = jnp.where(is_routed, e * capacity + slot_rank, -1).astype(jnp.float32)
     tables = jnp.stack([slot_of.T, scaling.T], axis=1)
-    got = [
+
+    even = e % 2 == 0
+    reach = jnp.where(even, owners - 1 - e, e)
+    pairs_a = [(s, s ^ 1) for s in range(owners)]
+    pairs_b = [(s, ((s + 1) ^ 1) - 1) for s in range(1, owners - 1)]
+
+    def gather_line(x):
+        from_a, from_b = [], []
+        for step in range(owners - 1):
+            a = lax.ppermute(x if step == 0 else from_b[step - 1], "expert", pairs_a)
+            if step < owners - 2:
+                from_b.append(lax.ppermute(x if step == 0 else from_a[step - 1], "expert", pairs_b))
+            from_a.append(a)
+        out = [x]
+        for k in range(1, owners):
+            got = from_a[k - 1]
+            for a in range(1, k, 2):
+                got = jnp.where(reach == a, from_b[k - a - 1], got)
+            out.append(got)
+        return out
+
+    def source(k):
+        way = jnp.where(even, 1, -1)
+        return jnp.where(k <= reach, e + way * k, e - way * (k - reach))
+
+    table_of = [lax.dynamic_index_in_dim(tables, e, 0, keepdims=False)]
+    by_turn = [table_of[0]] + [
         lax.ppermute(lax.dynamic_index_in_dim(tables, (e + k) % owners, 0, keepdims=False), "expert", turn(k))
-        if k
-        else lax.dynamic_index_in_dim(tables, e, 0, keepdims=False)
-        for k in range(owners)
+        for k in range(1, owners)
     ]
-    got = jnp.stack(got, axis=1)
-
-    chunks = CHUNKS
-    bounds, cuts = 0, []
-    for i in range(chunks):
-        cuts.append((i * tokens // chunks, (i + 1) * tokens // chunks))
-    order = jnp.concatenate([got[:, :, a:b].reshape(2, -1) for a, b in cuts], axis=1)
-    slot_id, scale = order[0].astype(jnp.int32), order[1]
-
-    def to_dp(j):
-        pairs = []
-        for src in range(n_dp):
-            for core in range(cores):
-                q = core * per_core + (src % per_core + j) % per_core
-                u = (src // per_core - core) % cores
-                pairs.append((src * cores + core, q * cores + u))
-        return pairs
-
-    def to_group(u_of, j):
-        pairs = []
-        for q in range(n_dp):
-            for core in range(cores):
-                d1 = u_of(core)
-                dest = ((q // per_core + d1) % cores) * per_core + (q % per_core - j) % per_core
-                pairs.append((q * cores + core, dest * cores + core))
-        return pairs
+    by_turn = jnp.stack(by_turn)
+    got = jnp.stack([by_turn[(e - source(k)) % owners] for k in range(owners)])
+    got = got.reshape(owners, 2, cores, part)
+    got = jnp.where(t == 0, got, got[:, :, ::-1])
+    got = got.transpose(1, 0, 2, 3).reshape(2, -1)
+    slot_id, scale = got[0].astype(jnp.int32), got[1]
 
     gate_pre = saved_gate.astype(jnp.float32)
     up_pre = saved_up.astype(jnp.float32)
@@ -134,49 +151,38 @@
         pick, activation, (((0,), (0,)), ((), ())), preferred_element_type=jnp.float32
     )
     in_tokens = (in_tokens * scale[:, None]).astype(jnp.bfloat16)
-
-    def from_group(u_of, j):
-        return [(b, a) for a, b in to_group(u_of, j)]
-
-    others = []
-    for x in range(1, cores + 1):
-        for j in range(per_core):
-            u_of = lambda core, x=x: (core + x) % cores
-            others.append(lax.ppermute(in_tokens, ("dp", "tensor"), from_group(u_of, j)))
-
-    mine_x, other_x, partial = [], [], []
-    for a, b in cuts:
-        first = []
-        for j in range(per_core):
-            block = lax.dynamic_slice(
-                out_grad, (jnp.int32(a), (p % per_core + j) % per_core * depth), (b - a, depth)
+    acts = {0: in_tokens}
+    for d in range(1, n_dp):
+        if d.bit_count() == 1:
+            acts[d] = over_dp(in_tokens, d)
+    for d in range(1, n_dp):
+        if d.bit_count() == 2:
+            low = d & -d
+            half = in_tokens.shape[0] // 2
+            acts[d] = jnp.concatenate(
+                [over_dp(acts[d - low][:half], low), over_dp(acts[low][half:], d - low)], axis=0
             )
-            first.append(lax.ppermute(block, ("dp", "tensor"), to_dp(j)))
-        first = jnp.stack(first)
-        rows = jnp.stack([first] + [lax.ppermute(first, "expert", turn(k)) for k in range(1, owners)], axis=1)
-        rows = rows.reshape(per_core, -1, depth)
-        mine_x.append(rows)
-        swapped = [
-            lax.ppermute(rows, "tensor", [(c, (c - x) % cores) for c in range(cores)]) for x in range(1, cores)
-        ]
-        other_x.append(swapped)
-        sums = None
-        for x in range(cores):
-            held = rows if x == 0 else swapped[x - 1]
-            for j in range(per_core):
-                piece = jnp.dot(held[j], weight, preferred_element_type=jnp.float32)
-                piece = piece.astype(jnp.bfloat16)
-                u_of = lambda core, x=x: (core + x) % cores
-                piece = lax.ppermute(piece, ("dp", "tensor"), to_group(u_of, j)).astype(jnp.float32)
-                sums = piece if sums is None else sums + piece
-        partial.append(sums)
-
-    total = jnp.concatenate(partial, axis=0) * scale[:, None]
+
+    lines = [gather_line(jnp.stack(blocks[d : d + n_dp // 2])) for d in (0, n_dp // 2)]
+    groups = [(0, 2)] + [(k, k + 1) for k in range(2, owners)]
+    held, sums = [], []
+    for a, b in groups:
+        mine = jnp.concatenate([jnp.stack(line[a:b], axis=1) for line in lines])
+        other = swap(mine)
+        rows = jnp.stack([mine, other], axis=2).reshape(n_dp, -1, depth)
+        held.append(rows)
+        total = jnp.dot(rows[0], weight, preferred_element_type=jnp.float32)
+        for d in range(1, n_dp):
+            piece = jnp.dot(rows[d], weight, preferred_element_type=jnp.float32).astype(jnp.bfloat16)
+            total += over_dp(piece, d).astype(jnp.float32)
+        sums.append(total)
+
+    total = jnp.concatenate(sums, axis=0) * scale[:, None]
     amax = jnp.max(jnp.abs(total)).reshape(1, 1)
-    grad_amax = lax.pmax(amax, "tensor")
-    high = total.astype(jnp.bfloat16)
-    low = (total - high.astype(jnp.float32)).astype(jnp.bfloat16)
-    grad_hidden = jnp.dot(pick, high, preferred_element_type=jnp.float32) + jnp.dot(
+    grad_amax = jnp.maximum(amax, swap(amax))
+    high = lax.reduce_precision(total, 8, 7)
+    low = (total - high).astype(jnp.bfloat16)
+    grad_hidden = jnp.dot(pick, high.astype(jnp.bfloat16), preferred_element_type=jnp.float32) + jnp.dot(
         pick, low, preferred_element_type=jnp.float32
     )
     quantized = (grad_hidden / (grad_amax + epsilon)).astype(jnp.bfloat16).astype(jnp.float32)
@@ -184,19 +190,12 @@
     grad_up = (quantized * silu_gate).astype(jnp.bfloat16)
 
     weight_sum = 0.0
-    for x in range(cores):
-        for j in range(per_core):
-            acts = others[(x - 1) % cores * per_core + j]
-            held = jnp.concatenate(
-                [(mine_x[i] if x == 0 else other_x[i][x - 1])[j] for i in range(chunks)], axis=0
-            )
-            weight_sum += lax.dot_general(
-                held, acts, (((0,), (0,)), ((), ())), preferred_element_type=jnp.float32
-            )
+    for d in range(n_dp):
+        rows = jnp.concatenate([rows[d] for rows in held], axis=0)
+        weight_sum += lax.dot_general(
+            rows, acts[d], (((0,), (0,)), ((), ())), preferred_element_type=jnp.float32
+        )
     return (weight_sum.astype(jnp.bfloat16).reshape(w_down.shape), grad_gate, grad_up, grad_amax)
-
-
-CHUNKS = 2
 
 
 def solution(mesh):
@@ -211,7 +210,8 @@
 
     def body(out_grad, routing, route_probs, w_down, saved_gate, saved_up):
         capacity = saved_gate.shape[0] // mesh.shape["expert"]
-        whole = capacity >= routing.shape[0] and mesh.shape["dp"] % mesh.shape["tensor"] == 0
+        n_dp, owners, cores = (mesh.shape[a] for a in ("dp", "expert", "tensor"))
+        whole = capacity >= routing.shape[0] and cores == 2 and owners % 2 == 0 and n_dp.bit_count() == 1 and n_dp >= cores
         return (by_tokens if whole else by_slots)(
             out_grad, routing, route_probs, w_down, saved_gate, saved_up
         )

time: 103 us -> 91.2 us (0.89)
  waiting for transfers between devices: 35.7 us -> 23.9 us
  blocking collectives: 3.08 us -> 0 us
  between operations: 1.69 us -> 3.43 us
  starting transfers between devices: 46.2 us -> 47.3 us
    ppermute x24 -> x31, waiting for transfers between devices: 35.7 us -> 21.7 us  [the longest x16 17 us: over_dp(): return lax.ppermute(x, 'dp', [(q, q ^ d) for q in range(n_dp)])]
    pmax x1 -> x0, blocking collectives: 3.08 us -> none  [by_tokens(): grad_amax = lax.pmax(amax, 'tensor')]
    ppermute x3, waiting for transfers between devices: 0.01 us -> 2.22 us  [by_tokens(): lax.ppermute(lax.dynamic_index_in_dim(tables, (e + k) % owners, 0, keepdi...]
    ppermute x24 -> x31, starting transfers between devices: 39.2 us -> 40.7 us  [the longest x6 19.1 us: gather_line(): a = lax.ppermute(x if step == 0 else from_b[step - 1], 'expert', pairs_a)]
    dot_general x13 -> x17, matrix products: 7.59 us -> 8.48 us  [the longest x4 3.65 us: by_tokens(): lax.dot_general(rows, acts[d], (((0,), (0,)), ((), ())), preferred_elemen...]
  transfers between devices with their start and end apart: 27 -> 34, of which waited for: 8 -> 9; matrix products, arithmetic and copies ran while one was open for 10% -> 12% of each run, Pallas kernels for 0% -> 0%
where the time goes in v2:
time: 91.2 us; the launch traced here: 90.9 us
  starting transfers between devices  47.3 us (52%)
  waiting for transfers between devices  23.9 us (26%)
  matrix products  11.2 us (12%)
  between operations  3.43 us (4%)
  other arithmetic  3.39 us (4%)
  local copies, waits for them, and re-layouts  1.57 us (2%)
    ppermute x6, starting transfers between devices, gather_line(): a = lax.ppermute(x if step == 0 else from_b[step - 1], 'expert', pairs_a)  19.1 us
    ppermute x16, starting transfers between devices, over_dp(): return lax.ppermute(x, 'dp', [(q, q ^ d) for q in range(n_dp)])  18.1 us
    ppermute x16, waiting for transfers between devices, over_dp(): return lax.ppermute(x, 'dp', [(q, q ^ d) for q in range(n_dp)])  17 us
    ppermute x3, starting transfers between devices, by_tokens(): lax.ppermute(lax.dynamic_index_in_dim(tables, (e + k) % owners, 0, keepdi...  6.64 us
    dot_general x4, matrix products, by_tokens(): lax.dot_general(rows, acts[d], (((0,), (0,)), ((), ())), preferred_elemen...  3.65 us
    ppermute x6, waiting for transfers between devices, gather_line(): a = lax.ppermute(x if step == 0 else from_b[step - 1], 'expert', pairs_a)  3.3 us
    dot_general x9, matrix products, by_tokens(): jnp.dot(rows[d], weight, preferred_element_type=jnp.float32)  3.18 us
    ppermute x4, starting transfers between devices, gather_line(): lax.ppermute(x if step == 0 else from_a[step - 1], 'expert', pairs_b)  2.67 us
  transfers between devices with their start and end apart: 34, of which 9 were waited for; matrix products, arithmetic and copies ran while one was open for 12% of the time, Pallas kernels for 0%

profile of v2, /device:TPU:0, one launch (start us, length us, event | category | flops | bytes accessed | tf_op | source)
XLA Modules:
  0.0 90.9 jit_solution(8136208689047563489)
XLA Ops:
  0.7 1.2 %constant_dynamic-slice_fusion.8 = (bf16[64,1792]{1,0:T(8,128)(2,1)S(1)}, bf16[64,1792]{1,0:T(8,128)(2,1)S(1)}) fusion(bf16[128,1792]{1,0:T(8,128)(2,1)} %param.6, s32[]{:T(128)S(6)} %select_n.146, s32[]{:T(128)S(6)} %select_n.147), kind=kLoop, calls=%fused_computation.159 | loop fusion | bytes 917512 | tf_op jit(solution)/shard_map/dynamic_slice | solution.py:94
  1.8 0.5 collective-permute-start
  2.3 0.8 fusion.101
  3.1 0.7 select_reduce_fusion
  4.0 2.7 %collective-permute-start.17 = (f32[2,128]{1,0:T(2,128)S(1)}, f32[2,128]{1,0:T(2,128)S(1)}, u32[]{:S(2)}, u32[]{:S(2)}) collective-permute-start(f32[2,128]{1,0:T(2,128)S(1)} %bitcast.159), channel_id=1, source_target_pairs={{0,2},{2,4},{4,6},{6,0},{1,3},{3,5},{5,7},{7,1},{8,10},{10,12},{12... | collective-permute-start | bytes 3080 | tf_op jit(solution)/shard_map/ppermute | solution.py:131
  6.7 2.6 %collective-permute-start.18 = (f32[2,128]{1,0:T(2,128)S(1)}, f32[2,128]{1,0:T(2,128)S(1)}, u32[]{:S(2)}, u32[]{:S(2)}) collective-permute-start(f32[2,128]{1,0:T(2,128)S(1)} %bitcast.158), channel_id=1, source_target_pairs={{0,4},{2,6},{4,0},{6,2},{1,5},{3,7},{5,1},{7,3},{8,12},{10,14},{12... | collective-permute-start | bytes 3080 | tf_op jit(solution)/shard_map/ppermute | solution.py:131
  9.3 1.3 %collective-permute-start.19 = (f32[2,128]{1,0:T(2,128)S(1)}, f32[2,128]{1,0:T(2,128)S(1)}, u32[]{:S(2)}, u32[]{:S(2)}) collective-permute-start(f32[2,128]{1,0:T(2,128)S(1)} %bitcast.157), channel_id=1, source_target_pairs={{0,6},{2,0},{4,2},{6,4},{1,7},{3,1},{5,3},{7,5},{8,14},{10,8},{12,... | collective-permute-start | bytes 3080 | tf_op jit(solution)/shard_map/ppermute | solution.py:131
  10.7 0.5 collective-permute-done.18
  11.2 1.7 %collective-permute-done.19 = f32[2,128]{1,0:T(2,128)S(1)} collective-permute-done((f32[2,128]{1,0:T(2,128)S(1)}, f32[2,128]{1,0:T(2,128)S(1)}, u32[]{:S(2)}, u32[]{:S(2)}) %collective-permute-start.19) | collective-permute-done | bytes 1056 | tf_op jit(solution)/shard_map/ppermute | solution.py:131
  13.3 1.6 %collective-permute-start.1 = (bf16[64,896]{1,0:T(8,128)(2,1)S(1)}, bf16[64,896]{1,0:T(8,128)(2,1)S(1)}, u32[]{:S(2)}, u32[]{:S(2)}) collective-permute-start(bf16[64,896]{1,0:T(8,128)(2,1)S(1)} %get-tuple-element.27), channel_id=1, source_target_pairs={{0,8},{8,0},{16,24},{24,16},{1,9},{9,1},{17,25},{25,17},{2,10},{10... | collective-permute-start | bytes 344072 | tf_op jit(solution)/shard_map/ppermute | solution.py:89
  14.8 1.5 %collective-permute-start.3 = (bf16[64,896]{1,0:T(8,128)(2,1)S(1)}, bf16[64,896]{1,0:T(8,128)(2,1)S(1)}, u32[]{:S(2)}, u32[]{:S(2)}) collective-permute-start(bf16[64,896]{1,0:T(8,128)(2,1)S(1)} %get-tuple-element.26), channel_id=1, source_target_pairs={{0,16},{8,24},{16,0},{24,8},{1,17},{9,25},{17,1},{25,9},{2,18},{10... | collective-permute-start | bytes 344072 | tf_op jit(solution)/shard_map/ppermute | solution.py:89
  16.3 0.5 collective-permute-start.4
  16.8 2.4 %collective-permute-done.1 = bf16[64,896]{1,0:T(8,128)(2,1)S(1)} collective-permute-done((bf16[64,896]{1,0:T(8,128)(2,1)S(1)}, bf16[64,896]{1,0:T(8,128)(2,1)S(1)}, u32[]{:S(2)}, u32[]{:S(2)}) %collective-permute-start.1) | collective-permute-done | bytes 114720 | tf_op jit(solution)/shard_map/ppermute | solution.py:89
  19.3 0.7 collective-permute-start.7
  20.2 0.5 collective-permute-done.3
  20.7 1.4 %collective-permute-done.4 = bf16[64,896]{1,0:T(8,128)(2,1)S(1)} collective-permute-done((bf16[64,896]{1,0:T(8,128)(2,1)S(1)}, bf16[64,896]{1,0:T(8,128)(2,1)S(1)}, u32[]{:S(2)}, u32[]{:S(2)}) %collective-permute-start.4) | collective-permute-done | bytes 114720 | tf_op jit(solution)/shard_map/ppermute | solution.py:89
  22.1 3.7 %collective-permute-start.5 = (bf16[2,64,896]{2,1,0:T(8,128)(2,1)S(1)}, bf16[2,64,896]{2,1,0:T(8,128)(2,1)S(1)}, u32[]{:S(2)}, u32[]{:S(2)}) collective-permute-start(bf16[2,64,896]{2,1,0:T(8,128)(2,1)S(1)} %get-tuple-element.33), channel_id=1, source_target_pairs={{0,2},{2,0},{4,6},{6,4},{1,3},{3,1},{5,7},{7,5},{8,10},{10,8},{12,... | collective-permute-start | bytes 688136 | tf_op jit(solution)/shard_map/ppermute | solution.py:113
  25.8 0.7 collective-permute-start.9
  26.4 5.4 %collective-permute-start.8 = (bf16[2,64,896]{2,1,0:T(8,128)(2,1)S(1)}, bf16[2,64,896]{2,1,0:T(8,128)(2,1)S(1)}, u32[]{:S(2)}, u32[]{:S(2)}) collective-permute-start(bf16[2,64,896]{2,1,0:T(8,128)(2,1)S(1)} %collective-permute-done.7), channel_id=1, source_target_pairs={{0,2},{2,0},{4,6},{6,4},{1,3},{3,1},{5,7},{7,5},{8,10},{10,8},{12,... | collective-permute-start | bytes 688136 | tf_op jit(solution)/shard_map/ppermute | solution.py:113
  31.8 0.7 collective-permute-start.12
  32.5 0.7 fusion
  33.2 1.0 %collective-permute-start.20 = (bf16[512,512]{1,0:T(8,128)(2,1)S(1)}, bf16[512,512]{1,0:T(8,128)(2,1)S(1)}, u32[]{:S(2)}, u32[]{:S(2)}) collective-permute-start(bf16[512,512]{1,0:T(8,128)(2,1)S(1)} %fusion), channel_id=1, source_target_pairs={{0,8},{8,0},{16,24},{24,16},{1,9},{9,1},{17,25},{25,17},{2,10},{10... | collective-permute-start | bytes 1572872 | tf_op jit(solution)/shard_map/ppermute | solution.py:89
  34.2 1.5 %collective-permute-start.21 = (bf16[512,512]{1,0:T(8,128)(2,1)S(1)}, bf16[512,512]{1,0:T(8,128)(2,1)S(1)}, u32[]{:S(2)}, u32[]{:S(2)}) collective-permute-start(bf16[512,512]{1,0:T(8,128)(2,1)S(1)} %fusion), channel_id=1, source_target_pairs={{0,16},{8,24},{16,0},{24,8},{1,17},{9,25},{17,1},{25,9},{2,18},{10... | collective-permute-start | bytes 1572872 | tf_op jit(solution)/shard_map/ppermute | solution.py:89
  35.7 2.5 %collective-permute-start.10 = (bf16[2,64,896]{2,1,0:T(8,128)(2,1)S(1)}, bf16[2,64,896]{2,1,0:T(8,128)(2,1)S(1)}, u32[]{:S(2)}, u32[]{:S(2)}) collective-permute-start(bf16[2,64,896]{2,1,0:T(8,128)(2,1)S(1)} %collective-permute-done.9), channel_id=1, source_target_pairs={{0,2},{2,0},{4,6},{6,4},{1,3},{3,1},{5,7},{7,5},{8,10},{10,8},{12,... | collective-permute-start | bytes 688136 | tf_op jit(solution)/shard_map/ppermute | solution.py:113
  38.3 0.7 collective-permute-start.14
  38.9 4.2 %collective-permute-start.13 = (bf16[2,64,896]{2,1,0:T(8,128)(2,1)S(1)}, bf16[2,64,896]{2,1,0:T(8,128)(2,1)S(1)}, u32[]{:S(2)}, u32[]{:S(2)}) collective-permute-start(bf16[2,64,896]{2,1,0:T(8,128)(2,1)S(1)} %collective-permute-done.12), channel_id=1, source_target_pairs={{0,2},{2,0},{4,6},{6,4},{1,3},{3,1},{5,7},{7,5},{8,10},{10,8},{12,... | collective-permute-start | bytes 688136 | tf_op jit(solution)/shard_map/ppermute | solution.py:113
  43.4 1.2 %collective-permute-start.22 = (bf16[256,512]{1,0:T(8,128)(2,1)S(1)}, bf16[256,512]{1,0:T(8,128)(2,1)S(1)}, u32[]{:S(2)}, u32[]{:S(2)}) collective-permute-start(bf16[256,512]{1,0:T(8,128)(2,1)S(1)} %slice.110), channel_id=1, source_target_pairs={{0,8},{8,0},{16,24},{24,16},{1,9},{9,1},{17,25},{25,17},{2,10},{10... | collective-permute-start | bytes 786440 | tf_op jit(solution)/shard_map/ppermute | solution.py:89
  44.6 0.1 maximum_maximum_fusion
  44.8 0.1 collective-permute-start.6
  44.9 3.3 %collective-permute-start.15 = (bf16[2,64,896]{2,1,0:T(8,128)(2,1)S(1)}, bf16[2,64,896]{2,1,0:T(8,128)(2,1)S(1)}, u32[]{:S(2)}, u32[]{:S(2)}) collective-permute-start(bf16[2,64,896]{2,1,0:T(8,128)(2,1)S(1)} %collective-permute-done.14), channel_id=1, source_target_pairs={{0,2},{2,0},{4,6},{6,4},{1,3},{3,1},{5,7},{7,5},{8,10},{10,8},{12,... | collective-permute-start | bytes 688136 | tf_op jit(solution)/shard_map/ppermute | solution.py:113
  48.4 0.3 convolution_convert_fusion.8
  48.7 0.3 collective-permute-start.27
  49.1 0.3 convolution_convert_fusion.7
  49.4 1.4 %collective-permute-start.28 = (bf16[128,512]{1,0:T(8,128)(2,1)S(1)}, bf16[128,512]{1,0:T(8,128)(2,1)S(1)}, u32[]{:S(2)}, u32[]{:S(2)}) collective-permute-start(bf16[128,512]{1,0:T(8,128)(2,1)S(1)} %convolution_convert_fusion.7), channel_id=1, source_target_pairs={{0,16},{8,24},{16,0},{24,8},{1,17},{9,25},{17,1},{25,9},{2,18},{10... | collective-permute-start | bytes 393224 | tf_op jit(solution)/shard_map/ppermute | solution.py:89
  50.8 0.3 convolution_convert_fusion.6
  51.1 3.3 %collective-permute-done.15 = bf16[2,64,896]{2,1,0:T(8,128)(2,1)S(1)} collective-permute-done((bf16[2,64,896]{2,1,0:T(8,128)(2,1)S(1)}, bf16[2,64,896]{2,1,0:T(8,128)(2,1)S(1)}, u32[]{:S(2)}, u32[]{:S(2)}) %collective-permute-start.15) | collective-permute-done | bytes 229408 | tf_op jit(solution)/shard_map/ppermute | solution.py:113
  54.4 1.1 %collective-permute-start.29 = (bf16[128,512]{1,0:T(8,128)(2,1)S(1)}, bf16[128,512]{1,0:T(8,128)(2,1)S(1)}, u32[]{:S(2)}, u32[]{:S(2)}) collective-permute-start(bf16[128,512]{1,0:T(8,128)(2,1)S(1)} %convolution_convert_fusion.6), channel_id=1, source_target_pairs={{0,24},{8,16},{16,8},{24,0},{1,25},{9,17},{17,9},{25,1},{2,26},{10... | collective-permute-start | bytes 393224 | tf_op jit(solution)/shard_map/ppermute | solution.py:89
  55.6 0.7 collective-permute-start.23
  56.4 4.3 %collective-permute-done.29 = bf16[128,512]{1,0:T(8,128)(2,1)S(1)} collective-permute-done((bf16[128,512]{1,0:T(8,128)(2,1)S(1)}, bf16[128,512]{1,0:T(8,128)(2,1)S(1)}, u32[]{:S(2)}, u32[]{:S(2)}) %collective-permute-start.29) | collective-permute-done | bytes 131104 | tf_op jit(solution)/shard_map/ppermute | solution.py:89
  60.7 0.3 fusion.72
  61.0 0.2 pad_maximum_fusion
  61.3 0.4 convolution_convert_fusion.2
  61.7 0.4 collective-permute-start.24
  62.1 0.4 convolution_convert_fusion.1
  62.6 1.3 %collective-permute-start.25 = (bf16[256,512]{1,0:T(8,128)(2,1)S(1)}, bf16[256,512]{1,0:T(8,128)(2,1)S(1)}, u32[]{:S(2)}, u32[]{:S(2)}) collective-permute-start(bf16[256,512]{1,0:T(8,128)(2,1)S(1)} %convolution_convert_fusion.1), channel_id=1, source_target_pairs={{0,16},{8,24},{16,0},{24,8},{1,17},{9,25},{17,1},{25,9},{2,18},{10... | collective-permute-start | bytes 786440 | tf_op jit(solution)/shard_map/ppermute | solution.py:89
  64.0 0.3 convolution_convert_fusion.5
  64.3 2.0 %collective-permute-start.30 = (bf16[128,512]{1,0:T(8,128)(2,1)S(1)}, bf16[128,512]{1,0:T(8,128)(2,1)S(1)}, u32[]{:S(2)}, u32[]{:S(2)}) collective-permute-start(bf16[128,512]{1,0:T(8,128)(2,1)S(1)} %convolution_convert_fusion.5), channel_id=1, source_target_pairs={{0,8},{8,0},{16,24},{24,16},{1,9},{9,1},{17,25},{25,17},{2,10},{10... | collective-permute-start | bytes 393224 | tf_op jit(solution)/shard_map/ppermute | solution.py:89
  66.4 0.7 fusion.16
  67.0 0.7 fusion.22
  67.7 0.7 fusion.28
  68.4 0.3 convolution_convert_fusion.4
  68.7 0.3 convolution_convert_fusion.3
  69.1 0.5 collective-permute-start.31
  69.6 1.1 %collective-permute-start.32 = (bf16[128,512]{1,0:T(8,128)(2,1)S(1)}, bf16[128,512]{1,0:T(8,128)(2,1)S(1)}, u32[]{:S(2)}, u32[]{:S(2)}) collective-permute-start(bf16[128,512]{1,0:T(8,128)(2,1)S(1)} %convolution_convert_fusion.3), channel_id=1, source_target_pairs={{0,24},{8,16},{16,8},{24,0},{1,25},{9,17},{17,9},{25,1},{2,26},{10... | collective-permute-start | bytes 393224 | tf_op jit(solution)/shard_map/ppermute | solution.py:89
  70.7 1.6 %fusion.15 = bf16[1,896,512]{2,1,0:T(8,128)(2,1)} fusion(f32[896,512]{1,0:T(8,128)S(1)} %fusion.28, f32[896,512]{1,0:T(8,128)S(1)} %fusion.16, f32[896,512]{1,0:T(8,128)S(1)} %fusion.22, bf16[128,896]{1,0:T(8,128)(2,1)S(1)} %bitcast.129, bf16[128,896]{1,0:T(8,128)(2,1)S(1)} %bitcast.127, bf16[256,896]{1,0:T(8,128)(2,1)S(1)} %bitcast.124, ...), kind=kOutput, calls=%fused_computation.59 | convolution fusion | flops 475398144 | bytes 7864320 | tf_op jit(solution)/shard_map/dot_general | solution.py:195
  72.3 0.4 convolution_convert_fusion
  72.7 1.9 %collective-permute-start.26 = (bf16[256,512]{1,0:T(8,128)(2,1)S(1)}, bf16[256,512]{1,0:T(8,128)(2,1)S(1)}, u32[]{:S(2)}, u32[]{:S(2)}) collective-permute-start(bf16[256,512]{1,0:T(8,128)(2,1)S(1)} %convolution_convert_fusion), channel_id=1, source_target_pairs={{0,24},{8,16},{16,8},{24,0},{1,25},{9,17},{17,9},{25,1},{2,26},{10... | collective-permute-start | bytes 786440 | tf_op jit(solution)/shard_map/ppermute | solution.py:89
  74.6 8.4 %collective-permute-done.31 = bf16[128,512]{1,0:T(8,128)(2,1)S(1)} collective-permute-done((bf16[128,512]{1,0:T(8,128)(2,1)S(1)}, bf16[128,512]{1,0:T(8,128)(2,1)S(1)}, u32[]{:S(2)}, u32[]{:S(2)}) %collective-permute-start.31) | collective-permute-done | bytes 131104 | tf_op jit(solution)/shard_map/ppermute | solution.py:89
  83.1 0.3 fusion.81
  83.4 0.5 fusion.63
  83.9 0.5 fusion.14
  84.4 0.8 abs_reduce_fusion
  85.2 1.4 %collective-permute-done.33 = f32[1,1]{1,0:T(1,128)} collective-permute-done((f32[1,1]{1,0:T(1,128)}, f32[1,1]{1,0:T(1,128)}, u32[]{:S(2)}, u32[]{:S(2)}) %collective-permute-start.33) | collective-permute-done | bytes 36 | tf_op jit(solution)/shard_map/ppermute | solution.py:92
  87.8 1.9 %fusion.8 = (bf16[512,512]{1,0:T(8,128)(2,1)}, bf16[512,512]{1,0:T(8,128)(2,1)}) fusion(bf16[512,512]{1,0:T(8,128)(2,1)S(1)} %copy-done.2, bf16[512,512]{1,0:T(8,128)(2,1)S(1)} %copy-done.1, f32[]{:T(128)} %bitcast.46, f32[512,512]{1,0:T(8,128)S(1)} %fusion.14, f32[512]{0:T(512)S(1)} %mul.91, f32[128,512]{1,0:T(8,128)S(1)} %fusion.81, ...), kind=kOutput, calls=%fused_computation.48 | convolution fusion | flops 275251200 | bytes 4198404 | tf_op jit(solution)/shard_map/dot_general | solution.py:185
  (60 shorter events, 1.5 us)
Async XLA Ops:
  0.6 47.8 %copy-start = (bf16[1,896,512]{2,1,0:T(8,128)(2,1)S(1)}, bf16[1,896,512]{2,1,0:T(8,128)(2,1)}, u32[]{:S(2)}) copy-start(bf16[1,896,512]{2,1,0:T(8,128)(2,1)} %param.9) | copy-start | bytes 2752516
  1.8 11.3 %collective-permute-start = (bf16[64,1792]{1,0:T(8,128)(2,1)S(1)}, bf16[64,1792]{1,0:T(8,128)(2,1)S(1)}, u32[]{:S(2)}, u32[]{:S(2)}) collective-permute-start(bf16[64,1792]{1,0:T(8,128)(2,1)S(1)} %get-tuple-element.29), channel_id=1, source_target_pairs={{0,1},{1,0},{2,3},{3,2},{4,5},{5,4},{6,7},{7,6},{8,9},{9,8},{10,11... | collective-permute-start | bytes 688136 | tf_op jit(solution)/shard_map/ppermute | solution.py:92
  2.3 30.2 %copy-start.1 = (bf16[512,512]{1,0:T(8,128)(2,1)S(1)}, bf16[512,512]{1,0:T(8,128)(2,1)}, u32[]{:S(2)}) copy-start(bf16[512,512]{1,0:T(8,128)(2,1)} %param.11) | copy-start | bytes 1572868
  2.3 30.2 %copy-start.2 = (bf16[512,512]{1,0:T(8,128)(2,1)S(1)}, bf16[512,512]{1,0:T(8,128)(2,1)}, u32[]{:S(2)}) copy-start(bf16[512,512]{1,0:T(8,128)(2,1)} %param.10) | copy-start | bytes 1572868
  4.0 6.6 %collective-permute-start.17 = (f32[2,128]{1,0:T(2,128)S(1)}, f32[2,128]{1,0:T(2,128)S(1)}, u32[]{:S(2)}, u32[]{:S(2)}) collective-permute-start(f32[2,128]{1,0:T(2,128)S(1)} %bitcast.159), channel_id=1, source_target_pairs={{0,2},{2,4},{4,6},{6,0},{1,3},{3,5},{5,7},{7,1},{8,10},{10,12},{12... | collective-permute-start | bytes 3080 | tf_op jit(solution)/shard_map/ppermute | solution.py:131
  6.7 4.5 %collective-permute-start.18 = (f32[2,128]{1,0:T(2,128)S(1)}, f32[2,128]{1,0:T(2,128)S(1)}, u32[]{:S(2)}, u32[]{:S(2)}) collective-permute-start(f32[2,128]{1,0:T(2,128)S(1)} %bitcast.158), channel_id=1, source_target_pairs={{0,4},{2,6},{4,0},{6,2},{1,5},{3,7},{5,1},{7,3},{8,12},{10,14},{12... | collective-permute-start | bytes 3080 | tf_op jit(solution)/shard_map/ppermute | solution.py:131
  9.3 3.6 %collective-permute-start.19 = (f32[2,128]{1,0:T(2,128)S(1)}, f32[2,128]{1,0:T(2,128)S(1)}, u32[]{:S(2)}, u32[]{:S(2)}) collective-permute-start(f32[2,128]{1,0:T(2,128)S(1)} %bitcast.157), channel_id=1, source_target_pairs={{0,6},{2,0},{4,2},{6,4},{1,7},{3,1},{5,3},{7,5},{8,14},{10,8},{12,... | collective-permute-start | bytes 3080 | tf_op jit(solution)/shard_map/ppermute | solution.py:131
  13.3 5.9 %collective-permute-start.1 = (bf16[64,896]{1,0:T(8,128)(2,1)S(1)}, bf16[64,896]{1,0:T(8,128)(2,1)S(1)}, u32[]{:S(2)}, u32[]{:S(2)}) collective-permute-start(bf16[64,896]{1,0:T(8,128)(2,1)S(1)} %get-tuple-element.27), channel_id=1, source_target_pairs={{0,8},{8,0},{16,24},{24,16},{1,9},{9,1},{17,25},{25,17},{2,10},{10... | collective-permute-start | bytes 344072 | tf_op jit(solution)/shard_map/ppermute | solution.py:89
  14.8 5.8 %collective-permute-start.3 = (bf16[64,896]{1,0:T(8,128)(2,1)S(1)}, bf16[64,896]{1,0:T(8,128)(2,1)S(1)}, u32[]{:S(2)}, u32[]{:S(2)}) collective-permute-start(bf16[64,896]{1,0:T(8,128)(2,1)S(1)} %get-tuple-element.26), channel_id=1, source_target_pairs={{0,16},{8,24},{16,0},{24,8},{1,17},{9,25},{17,1},{25,9},{2,18},{10... | collective-permute-start | bytes 344072 | tf_op jit(solution)/shard_map/ppermute | solution.py:89
  16.3 5.7 %collective-permute-start.4 = (bf16[64,896]{1,0:T(8,128)(2,1)S(1)}, bf16[64,896]{1,0:T(8,128)(2,1)S(1)}, u32[]{:S(2)}, u32[]{:S(2)}) collective-permute-start(bf16[64,896]{1,0:T(8,128)(2,1)S(1)} %get-tuple-element.25), channel_id=1, source_target_pairs={{0,24},{8,16},{16,8},{24,0},{1,25},{9,17},{17,9},{25,1},{2,26},{10... | collective-permute-start | bytes 344072 | tf_op jit(solution)/shard_map/ppermute | solution.py:89
  19.2 12.6 %collective-permute-start.2 = (bf16[2,64,896]{2,1,0:T(8,128)(2,1)S(1)}, bf16[2,64,896]{2,1,0:T(8,128)(2,1)S(1)}, u32[]{:S(2)}, u32[]{:S(2)}) collective-permute-start(bf16[2,64,896]{2,1,0:T(8,128)(2,1)S(1)} %get-tuple-element.31), channel_id=1, source_target_pairs={{0,2},{2,0},{4,6},{6,4},{1,3},{3,1},{5,7},{7,5},{8,10},{10,8},{12,... | collective-permute-start | bytes 688136 | tf_op jit(solution)/shard_map/ppermute | solution.py:113
  19.3 7.1 %collective-permute-start.7 = (bf16[2,64,896]{2,1,0:T(8,128)(2,1)S(1)}, bf16[2,64,896]{2,1,0:T(8,128)(2,1)S(1)}, u32[]{:S(2)}, u32[]{:S(2)}) collective-permute-start(bf16[2,64,896]{2,1,0:T(8,128)(2,1)S(1)} %get-tuple-element.31), channel_id=1, source_target_pairs={{2,4},{4,2},{3,5},{5,3},{10,12},{12,10},{11,13},{13,11},{18,20},{2... | collective-permute-start | bytes 688136 | tf_op jit(solution)/shard_map/ppermute | solution.py:115
  22.1 12.1 %collective-permute-start.5 = (bf16[2,64,896]{2,1,0:T(8,128)(2,1)S(1)}, bf16[2,64,896]{2,1,0:T(8,128)(2,1)S(1)}, u32[]{:S(2)}, u32[]{:S(2)}) collective-permute-start(bf16[2,64,896]{2,1,0:T(8,128)(2,1)S(1)} %get-tuple-element.33), channel_id=1, source_target_pairs={{0,2},{2,0},{4,6},{6,4},{1,3},{3,1},{5,7},{7,5},{8,10},{10,8},{12,... | collective-permute-start | bytes 688136 | tf_op jit(solution)/shard_map/ppermute | solution.py:113
  25.8 10.0 %collective-permute-start.9 = (bf16[2,64,896]{2,1,0:T(8,128)(2,1)S(1)}, bf16[2,64,896]{2,1,0:T(8,128)(2,1)S(1)}, u32[]{:S(2)}, u32[]{:S(2)}) collective-permute-start(bf16[2,64,896]{2,1,0:T(8,128)(2,1)S(1)} %get-tuple-element.33), channel_id=1, source_target_pairs={{2,4},{4,2},{3,5},{5,3},{10,12},{12,10},{11,13},{13,11},{18,20},{2... | collective-permute-start | bytes 688136 | tf_op jit(solution)/shard_map/ppermute | solution.py:115
  26.4 11.8 %collective-permute-start.8 = (bf16[2,64,896]{2,1,0:T(8,128)(2,1)S(1)}, bf16[2,64,896]{2,1,0:T(8,128)(2,1)S(1)}, u32[]{:S(2)}, u32[]{:S(2)}) collective-permute-start(bf16[2,64,896]{2,1,0:T(8,128)(2,1)S(1)} %collective-permute-done.7), channel_id=1, source_target_pairs={{0,2},{2,0},{4,6},{6,4},{1,3},{3,1},{5,7},{7,5},{8,10},{10,8},{12,... | collective-permute-start | bytes 688136 | tf_op jit(solution)/shard_map/ppermute | solution.py:113
  31.8 7.1 %collective-permute-start.12 = (bf16[2,64,896]{2,1,0:T(8,128)(2,1)S(1)}, bf16[2,64,896]{2,1,0:T(8,128)(2,1)S(1)}, u32[]{:S(2)}, u32[]{:S(2)}) collective-permute-start(bf16[2,64,896]{2,1,0:T(8,128)(2,1)S(1)} %collective-permute-done.2), channel_id=1, source_target_pairs={{2,4},{4,2},{3,5},{5,3},{10,12},{12,10},{11,13},{13,11},{18,20},{2... | collective-permute-start | bytes 688136 | tf_op jit(solution)/shard_map/ppermute | solution.py:115
  33.2 11.4 %collective-permute-start.20 = (bf16[512,512]{1,0:T(8,128)(2,1)S(1)}, bf16[512,512]{1,0:T(8,128)(2,1)S(1)}, u32[]{:S(2)}, u32[]{:S(2)}) collective-permute-start(bf16[512,512]{1,0:T(8,128)(2,1)S(1)} %fusion), channel_id=1, source_target_pairs={{0,8},{8,0},{16,24},{24,16},{1,9},{9,1},{17,25},{25,17},{2,10},{10... | collective-permute-start | bytes 1572872 | tf_op jit(solution)/shard_map/ppermute | solution.py:89
  34.2 9.2 %collective-permute-start.21 = (bf16[512,512]{1,0:T(8,128)(2,1)S(1)}, bf16[512,512]{1,0:T(8,128)(2,1)S(1)}, u32[]{:S(2)}, u32[]{:S(2)}) collective-permute-start(bf16[512,512]{1,0:T(8,128)(2,1)S(1)} %fusion), channel_id=1, source_target_pairs={{0,16},{8,24},{16,0},{24,8},{1,17},{9,25},{17,1},{25,9},{2,18},{10... | collective-permute-start | bytes 1572872 | tf_op jit(solution)/shard_map/ppermute | solution.py:89
  35.7 7.4 %collective-permute-start.10 = (bf16[2,64,896]{2,1,0:T(8,128)(2,1)S(1)}, bf16[2,64,896]{2,1,0:T(8,128)(2,1)S(1)}, u32[]{:S(2)}, u32[]{:S(2)}) collective-permute-start(bf16[2,64,896]{2,1,0:T(8,128)(2,1)S(1)} %collective-permute-done.9), channel_id=1, source_target_pairs={{0,2},{2,0},{4,6},{6,4},{1,3},{3,1},{5,7},{7,5},{8,10},{10,8},{12,... | collective-permute-start | bytes 688136 | tf_op jit(solution)/shard_map/ppermute | solution.py:113
  38.3 6.7 %collective-permute-start.14 = (bf16[2,64,896]{2,1,0:T(8,128)(2,1)S(1)}, bf16[2,64,896]{2,1,0:T(8,128)(2,1)S(1)}, u32[]{:S(2)}, u32[]{:S(2)}) collective-permute-start(bf16[2,64,896]{2,1,0:T(8,128)(2,1)S(1)} %collective-permute-done.5), channel_id=1, source_target_pairs={{2,4},{4,2},{3,5},{5,3},{10,12},{12,10},{11,13},{13,11},{18,20},{2... | collective-permute-start | bytes 688136 | tf_op jit(solution)/shard_map/ppermute | solution.py:115
  38.9 9.3 %collective-permute-start.13 = (bf16[2,64,896]{2,1,0:T(8,128)(2,1)S(1)}, bf16[2,64,896]{2,1,0:T(8,128)(2,1)S(1)}, u32[]{:S(2)}, u32[]{:S(2)}) collective-permute-start(bf16[2,64,896]{2,1,0:T(8,128)(2,1)S(1)} %collective-permute-done.12), channel_id=1, source_target_pairs={{0,2},{2,0},{4,6},{6,4},{1,3},{3,1},{5,7},{7,5},{8,10},{10,8},{12,... | collective-permute-start | bytes 688136 | tf_op jit(solution)/shard_map/ppermute | solution.py:113
  43.3 5.0 %collective-permute-start.11 = (bf16[4,1,64,896]{3,2,0,1:T(8,128)(2,1)S(1)}, bf16[4,1,64,896]{3,2,0,1:T(8,128)(2,1)S(1)}, u32[]{:S(2)}, u32[]{:S(2)}) collective-permute-start(bf16[4,1,64,896]{3,2,0,1:T(8,128)(2,1)S(1)} %get-tuple-element.20), channel_id=1, source_target_pairs={{0,1},{1,0},{2,3},{3,2},{4,5},{5,4},{6,7},{7,6},{8,9},{9,8},{10,11... | collective-permute-start | bytes 1376264 | tf_op jit(solution)/shard_map/ppermute | solution.py:92
  43.4 25.6 %collective-permute-start.22 = (bf16[256,512]{1,0:T(8,128)(2,1)S(1)}, bf16[256,512]{1,0:T(8,128)(2,1)S(1)}, u32[]{:S(2)}, u32[]{:S(2)}) collective-permute-start(bf16[256,512]{1,0:T(8,128)(2,1)S(1)} %slice.110), channel_id=1, source_target_pairs={{0,8},{8,0},{16,24},{24,16},{1,9},{9,1},{17,25},{25,17},{2,10},{10... | collective-permute-start | bytes 786440 | tf_op jit(solution)/shard_map/ppermute | solution.py:89
  44.8 16.2 %collective-permute-start.6 = (bf16[4,2,64,896]{3,2,1,0:T(8,128)(2,1)S(1)}, bf16[4,2,64,896]{3,2,1,0:T(8,128)(2,1)S(1)}, u32[]{:S(2)}, u32[]{:S(2)}) collective-permute-start(bf16[4,2,64,896]{3,2,1,0:T(8,128)(2,1)S(1)} %get-tuple-element.18), channel_id=1, source_target_pairs={{0,1},{1,0},{2,3},{3,2},{4,5},{5,4},{6,7},{7,6},{8,9},{9,8},{10,11... | collective-permute-start | bytes 2752520 | tf_op jit(solution)/shard_map/ppermute | solution.py:92
  44.9 9.5 %collective-permute-start.15 = (bf16[2,64,896]{2,1,0:T(8,128)(2,1)S(1)}, bf16[2,64,896]{2,1,0:T(8,128)(2,1)S(1)}, u32[]{:S(2)}, u32[]{:S(2)}) collective-permute-start(bf16[2,64,896]{2,1,0:T(8,128)(2,1)S(1)} %collective-permute-done.14), channel_id=1, source_target_pairs={{0,2},{2,0},{4,6},{6,4},{1,3},{3,1},{5,7},{7,5},{8,10},{10,8},{12,... | collective-permute-start | bytes 688136 | tf_op jit(solution)/shard_map/ppermute | solution.py:113
  48.7 6.9 %collective-permute-start.27 = (bf16[128,512]{1,0:T(8,128)(2,1)S(1)}, bf16[128,512]{1,0:T(8,128)(2,1)S(1)}, u32[]{:S(2)}, u32[]{:S(2)}) collective-permute-start(bf16[128,512]{1,0:T(8,128)(2,1)S(1)} %convolution_convert_fusion.8), channel_id=1, source_target_pairs={{0,8},{8,0},{16,24},{24,16},{1,9},{9,1},{17,25},{25,17},{2,10},{10... | collective-permute-start | bytes 393224 | tf_op jit(solution)/shard_map/ppermute | solution.py:89
  49.4 7.0 %collective-permute-start.28 = (bf16[128,512]{1,0:T(8,128)(2,1)S(1)}, bf16[128,512]{1,0:T(8,128)(2,1)S(1)}, u32[]{:S(2)}, u32[]{:S(2)}) collective-permute-start(bf16[128,512]{1,0:T(8,128)(2,1)S(1)} %convolution_convert_fusion.7), channel_id=1, source_target_pairs={{0,16},{8,24},{16,0},{24,8},{1,17},{9,25},{17,1},{25,9},{2,18},{10... | collective-permute-start | bytes 393224 | tf_op jit(solution)/shard_map/ppermute | solution.py:89
  54.4 6.3 %collective-permute-start.29 = (bf16[128,512]{1,0:T(8,128)(2,1)S(1)}, bf16[128,512]{1,0:T(8,128)(2,1)S(1)}, u32[]{:S(2)}, u32[]{:S(2)}) collective-permute-start(bf16[128,512]{1,0:T(8,128)(2,1)S(1)} %convolution_convert_fusion.6), channel_id=1, source_target_pairs={{0,24},{8,16},{16,8},{24,0},{1,25},{9,17},{17,9},{25,1},{2,26},{10... | collective-permute-start | bytes 393224 | tf_op jit(solution)/shard_map/ppermute | solution.py:89
  55.6 14.0 %collective-permute-start.23 = (bf16[256,512]{1,0:T(8,128)(2,1)S(1)}, bf16[256,512]{1,0:T(8,128)(2,1)S(1)}, u32[]{:S(2)}, u32[]{:S(2)}) collective-permute-start(bf16[256,512]{1,0:T(8,128)(2,1)S(1)} %slice.111), channel_id=1, source_target_pairs={{0,16},{8,24},{16,0},{24,8},{1,17},{9,25},{17,1},{25,9},{2,18},{10... | collective-permute-start | bytes 786440 | tf_op jit(solution)/shard_map/ppermute | solution.py:89
  56.4 7.6 %collective-permute-start.16 = (bf16[4,1,64,896]{3,2,0,1:T(8,128)(2,1)S(1)}, bf16[4,1,64,896]{3,2,0,1:T(8,128)(2,1)S(1)}, u32[]{:S(2)}, u32[]{:S(2)}) collective-permute-start(bf16[4,1,64,896]{3,2,0,1:T(8,128)(2,1)S(1)} %get-tuple-element.22), channel_id=1, source_target_pairs={{0,1},{1,0},{2,3},{3,2},{4,5},{5,4},{6,7},{7,6},{8,9},{9,8},{10,11... | collective-permute-start | bytes 1376264 | tf_op jit(solution)/shard_map/ppermute | solution.py:92
  61.7 21.7 %collective-permute-start.24 = (bf16[256,512]{1,0:T(8,128)(2,1)S(1)}, bf16[256,512]{1,0:T(8,128)(2,1)S(1)}, u32[]{:S(2)}, u32[]{:S(2)}) collective-permute-start(bf16[256,512]{1,0:T(8,128)(2,1)S(1)} %convolution_convert_fusion.2), channel_id=1, source_target_pairs={{0,8},{8,0},{16,24},{24,16},{1,9},{9,1},{17,25},{25,17},{2,10},{10... | collective-permute-start | bytes 786440 | tf_op jit(solution)/shard_map/ppermute | solution.py:89
  62.6 20.8 %collective-permute-start.25 = (bf16[256,512]{1,0:T(8,128)(2,1)S(1)}, bf16[256,512]{1,0:T(8,128)(2,1)S(1)}, u32[]{:S(2)}, u32[]{:S(2)}) collective-permute-start(bf16[256,512]{1,0:T(8,128)(2,1)S(1)} %convolution_convert_fusion.1), channel_id=1, source_target_pairs={{0,16},{8,24},{16,0},{24,8},{1,17},{9,25},{17,1},{25,9},{2,18},{10... | collective-permute-start | bytes 786440 | tf_op jit(solution)/shard_map/ppermute | solution.py:89
  64.3 8.4 %collective-permute-start.30 = (bf16[128,512]{1,0:T(8,128)(2,1)S(1)}, bf16[128,512]{1,0:T(8,128)(2,1)S(1)}, u32[]{:S(2)}, u32[]{:S(2)}) collective-permute-start(bf16[128,512]{1,0:T(8,128)(2,1)S(1)} %convolution_convert_fusion.5), channel_id=1, source_target_pairs={{0,8},{8,0},{16,24},{24,16},{1,9},{9,1},{17,25},{25,17},{2,10},{10... | collective-permute-start | bytes 393224 | tf_op jit(solution)/shard_map/ppermute | solution.py:89
  69.1 14.0 %collective-permute-start.31 = (bf16[128,512]{1,0:T(8,128)(2,1)S(1)}, bf16[128,512]{1,0:T(8,128)(2,1)S(1)}, u32[]{:S(2)}, u32[]{:S(2)}) collective-permute-start(bf16[128,512]{1,0:T(8,128)(2,1)S(1)} %convolution_convert_fusion.4), channel_id=1, source_target_pairs={{0,16},{8,24},{16,0},{24,8},{1,17},{9,25},{17,1},{25,9},{2,18},{10... | collective-permute-start | bytes 393224 | tf_op jit(solution)/shard_map/ppermute | solution.py:89
  69.6 13.4 %collective-permute-start.32 = (bf16[128,512]{1,0:T(8,128)(2,1)S(1)}, bf16[128,512]{1,0:T(8,128)(2,1)S(1)}, u32[]{:S(2)}, u32[]{:S(2)}) collective-permute-start(bf16[128,512]{1,0:T(8,128)(2,1)S(1)} %convolution_convert_fusion.3), channel_id=1, source_target_pairs={{0,24},{8,16},{16,8},{24,0},{1,25},{9,17},{17,9},{25,1},{2,26},{10... | collective-permute-start | bytes 393224 | tf_op jit(solution)/shard_map/ppermute | solution.py:89
  72.7 10.7 %collective-permute-start.26 = (bf16[256,512]{1,0:T(8,128)(2,1)S(1)}, bf16[256,512]{1,0:T(8,128)(2,1)S(1)}, u32[]{:S(2)}, u32[]{:S(2)}) collective-permute-start(bf16[256,512]{1,0:T(8,128)(2,1)S(1)} %convolution_convert_fusion), channel_id=1, source_target_pairs={{0,24},{8,16},{16,8},{24,0},{1,25},{9,17},{17,9},{25,1},{2,26},{10... | collective-permute-start | bytes 786440 | tf_op jit(solution)/shard_map/ppermute | solution.py:89
  85.2 1.4 %collective-permute-start.33 = (f32[1,1]{1,0:T(1,128)}, f32[1,1]{1,0:T(1,128)}, u32[]{:S(2)}, u32[]{:S(2)}) collective-permute-start(f32[1,1]{1,0:T(1,128)} %bitcast.45), channel_id=1, source_target_pairs={{0,1},{1,0},{2,3},{3,2},{4,5},{5,4},{6,7},{7,6},{8,9},{9,8},{10,11... | collective-permute-start | bytes 20 | tf_op jit(solution)/shard_map/ppermute | solution.py:92
